TPU v7x, 32 devices: a whole 2x2x4 slice. The times are simulated.
32 devices in a mesh: dp: 4 (over x, core), expert: 8 (over z, y).
Axes of the slice: x: 2, y: 2, z: 4, core: 2. Of those that a mesh axis runs over, the one named last changes fastest.
Arguments:
- tokens: bfloat16 [4096, 768], P(('dp', 'expert')), may hold values from -6 to 6
- cotangent: bfloat16 [4096, 768], P(('dp', 'expert')), may hold values from -6 to 6
- doc_ids: int32 [64, 64], P(('dp', 'expert')), may hold values from 0 to 2, never falling along the last dimension, each value on 1 to 48 neighbouring positions
- expert_ids: int32 [4096, 2], P(('dp', 'expert')), may hold values from 0 to 31, all different within a row; in each aligned block of 64 rows (0 to 63, 64 to 127, ...) at most 5 rows name the same one
- gate_logits: float32 [4096, 2], P(('dp', 'expert')), may hold values from -6 to 6
- gain_attn_a: bfloat16 [768], P(('dp', 'expert')), may hold values from 0.5 to 1.5
- gain_mlp: bfloat16 [768], P(('dp', 'expert')), may hold values from 0.5 to 1.5
- gain_attn_b: bfloat16 [768], P(('dp', 'expert')), may hold values from 0.5 to 1.5
- gain_moe: bfloat16 [768], P(('dp', 'expert')), may hold values from 0.5 to 1.5
- bias_a: bfloat16 [384], P(('dp', 'expert')), may hold values from -4 to 4
- bias_b: bfloat16 [384], P(('dp', 'expert')), may hold values from -4 to 4
- qkv_a: bfloat16 [768, 2304], P(('dp', 'expert')), may hold values from -0.21875 to 0.21875
- out_a: bfloat16 [768, 768], P(('dp', 'expert')), may hold values from -0.875 to 0.875
- w_gate: bfloat16 [768, 3072], P(('dp', 'expert')), may hold values from -0.21875 to 0.21875
- w_up: bfloat16 [768, 3072], P(('dp', 'expert')), may hold values from -0.21875 to 0.21875
- w_down: bfloat16 [3072, 768], P(('dp', 'expert')), may hold values from -0.15625 to 0.15625
- qkv_b: bfloat16 [768, 2304], P(('dp', 'expert')), may hold values from -0.21875 to 0.21875
- out_b: bfloat16 [768, 768], P(('dp', 'expert')), may hold values from -0.875 to 0.875
- expert_in: bfloat16 [32, 768, 3072], P('expert', None, 'dp'), may hold values from -0.21875 to 0.21875
- expert_out: bfloat16 [32, 3072, 768], P('expert', 'dp'), may hold values from -0.15625 to 0.15625
Outputs:
- out: bfloat16 [4096, 768], P(('dp', 'expert'))
- grad_tokens: float32 [4096, 768], P(('dp', 'expert'))
- grad_gain_attn_a: float32 [768], P(('dp', 'expert'))
- grad_gain_mlp: float32 [768], P(('dp', 'expert'))
- grad_gain_attn_b: float32 [768], P(('dp', 'expert'))
- grad_gain_moe: float32 [768], P(('dp', 'expert'))
- grad_bias_a: float32 [384], P(('dp', 'expert'))
- grad_bias_b: float32 [384], P(('dp', 'expert'))
- grad_qkv_a: float32 [768, 2304], P(('dp', 'expert'))
- grad_out_a: float32 [768, 768], P(('dp', 'expert'))
- grad_w_gate: float32 [768, 3072], P(('dp', 'expert'))
- grad_w_up: float32 [768, 3072], P(('dp', 'expert'))
- grad_w_down: float32 [3072, 768], P(('dp', 'expert'))
- grad_qkv_b: float32 [768, 2304], P(('dp', 'expert'))
- grad_out_b: float32 [768, 768], P(('dp', 'expert'))
- grad_expert_in: float32 [32, 768, 3072], P('expert', None, 'dp')
- grad_expert_out: float32 [32, 3072, 768], P('expert', 'dp')
Inputs may be any that keep to these rules, and one draw needn't show every extreme that they name: `expert_ids`: each row names two different experts; in each aligned block of 64 rows (one micro-batch of one device) no expert is named by more than 5 rows, a bound that some block reaches. `doc_ids`: within each row, document numbers never fall; a document holds 1 to 64 - 64 // 4 positions, and one holds exactly that many.
All inputs are finite; a program needn't handle non-finite values.
Results may differ from a plain program's by a relative error of at most 0.02.
Values may be sent and summed in bfloat16 or wider, within the bound.
A program may use at most 256 MiB of HBM per device.

v0:
```python
import math

import jax
import jax.numpy as jnp
from jax import lax
from jax.sharding import PartitionSpec as P

D = 768
HEADS = 12
HEAD_DIM = 64
BUCKETS = 32
EXP_DEV = 4
ROWS = 64
MICRO = 2


EPSILON = 1e-06
HIGH = lax.Precision.HIGHEST
ROOT_HALF = 0.7071067811865476
ROOT_TWO_PI = 0.3989422804014327


def for_sending(value):
    return jax.tree.map(lambda a: a.astype(jnp.bfloat16) if a.dtype == jnp.float32 else a, value)


def product(left, right):
    return jnp.dot(left, right, preferred_element_type=jnp.float32)


def product_left(left, right):
    return lax.dot_general(
        left, right, (((0,), (0,)), ((), ())), preferred_element_type=jnp.float32
    )


def product_right(left, right):
    return lax.dot_general(
        left, right, (((1,), (1,)), ((), ())), preferred_element_type=jnp.float32
    )


def gelu_slope(values):
    return (
        0.5 * (1.0 + lax.erf(values * ROOT_HALF))
        + values * jnp.exp(-0.5 * values * values) * ROOT_TWO_PI
    )


def normalize(rows, gain):
    scale = lax.rsqrt(jnp.mean(rows * rows, axis=-1, keepdims=True) + EPSILON)
    return (rows * scale * gain, scale)


def norm_back(grad, rows, scale, gain):
    unit = rows * scale
    grad_gain = jnp.sum(grad * unit, axis=0)
    inner = grad * gain
    return (scale * (inner - unit * jnp.mean(inner * unit, axis=-1, keepdims=True)), grad_gain)


def layout(docs):
    count = docs.shape[0]
    place = jnp.arange(count, dtype=jnp.int32)
    apart = place[:, None] - place[None, :]
    allowed = (apart >= 0) & (docs[:, None] == docs[None, :])
    bucket = jnp.clip(apart, 0, BUCKETS - 1)
    table = (bucket[:, :, None] == jnp.arange(BUCKETS, dtype=jnp.int32)[None, None, :]).astype(
        jnp.float32
    )
    return (allowed, table)


def score_of(queries, keys, bias, allowed, table):
    scores = jnp.einsum("qhd,khd->hqk", queries, keys, preferred_element_type=jnp.float32) * (
        1.0 / math.sqrt(HEAD_DIM)
    )
    scores = scores + jnp.einsum("hb,qkb->hqk", bias, table, precision=HIGH)
    return jnp.where(allowed[None], scores, -1000000000.0)


def attention_forward(rows, gain, bias, wqkv, wout, allowed, table):
    count = rows.shape[0]
    normed_full, scale = normalize(rows, gain)
    normed = normed_full.astype(jnp.bfloat16)
    mixed = product(normed, wqkv).astype(jnp.bfloat16).reshape(count, 3, HEADS, HEAD_DIM)
    queries, keys, values = (mixed[:, 0], mixed[:, 1], mixed[:, 2])
    scores = score_of(queries, keys, bias, allowed, table)
    top = jnp.max(scores, axis=-1, keepdims=True)
    total = jnp.sum(jnp.exp(scores - top), axis=-1, keepdims=True)
    summit = top + jnp.log(total)
    attend = jnp.exp(scores - summit)
    context = jnp.einsum(
        "hqk,khd->qhd", attend.astype(jnp.bfloat16), values, preferred_element_type=jnp.float32
    )
    context = context.reshape(count, D).astype(jnp.bfloat16)
    return (product(context, wout), (scale, normed, queries, keys, values, context, summit))


def attention_back(grad, rows, gain, bias, wqkv, wout, allowed, table, kept):
    scale, normed, queries, keys, values, context, summit = kept
    count = rows.shape[0]
    grad_low = grad.astype(jnp.bfloat16)
    grad_context = (
        product_right(grad_low, wout).astype(jnp.bfloat16).reshape(count, HEADS, HEAD_DIM)
    )
    attend = jnp.exp(score_of(queries, keys, bias, allowed, table) - summit)
    grad_values = jnp.einsum(
        "hqk,qhd->khd",
        attend.astype(jnp.bfloat16),
        grad_context,
        preferred_element_type=jnp.float32,
    )
    grad_attend = jnp.einsum(
        "qhd,khd->hqk", grad_context, values, preferred_element_type=jnp.float32
    )
    grad_scores = attend * (grad_attend - jnp.sum(attend * grad_attend, axis=-1, keepdims=True))
    scores_low = grad_scores.astype(jnp.bfloat16)
    grad_bias = jnp.einsum("hqk,qkb->hb", scores_low.astype(jnp.float32), table, precision=HIGH)
    factor = 1.0 / math.sqrt(HEAD_DIM)
    grad_queries = (
        jnp.einsum("hqk,khd->qhd", scores_low, keys, preferred_element_type=jnp.float32) * factor
    )
    grad_keys = (
        jnp.einsum("hqk,qhd->khd", scores_low, queries, preferred_element_type=jnp.float32) * factor
    )
    grad_mixed = (
        jnp.stack([grad_queries, grad_keys, grad_values], axis=1)
        .reshape(count, 3 * D)
        .astype(jnp.bfloat16)
    )
    grad_normed = product_right(grad_mixed, wqkv)
    grad_rows, grad_gain = norm_back(grad_normed, rows, scale, gain)
    return (
        grad_rows,
        (grad_gain, grad_bias.reshape(-1), (normed, grad_mixed), (context, grad_low)),
    )


def feed_forward(rows, gain, w_gate, w_up, w_down):
    normed_full, scale = normalize(rows, gain)
    normed = normed_full.astype(jnp.bfloat16)
    gate = product(normed, w_gate)
    up_part = product(normed, w_up)
    hidden = (jax.nn.gelu(gate, approximate=False) * up_part).astype(jnp.bfloat16)
    return (product(hidden, w_down), (scale, normed, gate, up_part, hidden))


def feed_back(grad, rows, gain, w_gate, w_up, w_down, kept):
    scale, normed, gate, up_part, hidden = kept
    grad_low = grad.astype(jnp.bfloat16)
    grad_hidden = product_right(grad_low, w_down)
    grad_gate = (grad_hidden * up_part * gelu_slope(gate)).astype(jnp.bfloat16)
    grad_up = (grad_hidden * jax.nn.gelu(gate, approximate=False)).astype(jnp.bfloat16)
    grad_normed = product_right(grad_gate, w_gate) + product_right(grad_up, w_up)
    grad_rows, grad_gain = norm_back(grad_normed, rows, scale, gain)
    return (grad_rows, (grad_gain, (normed, grad_gate), (normed, grad_up), (hidden, grad_low)))


def route_table(ids, experts, capacity):
    flat = ids.reshape(-1)
    hits = (flat[:, None] == jnp.arange(experts, dtype=jnp.int32)[None, :]).astype(jnp.int32)
    before = jnp.cumsum(hits, axis=0) - hits
    slot = jnp.sum(before * hits, axis=1)
    target = slot * experts + flat
    return (target[:, None] == jnp.arange(capacity * experts, dtype=jnp.int32)[None, :]).astype(
        jnp.bfloat16
    )


def weight_grad(pairs):
    left = jnp.concatenate([item[0] for item in pairs], axis=0)
    right = jnp.concatenate([item[1] for item in pairs], axis=0)
    return product_left(left, right)


def body(
    tokens,
    cotangent,
    doc_ids,
    expert_ids,
    gate_logits,
    gain_attn_a,
    gain_mlp,
    gain_attn_b,
    gain_moe,
    bias_a,
    bias_b,
    qkv_a,
    out_a,
    w_gate,
    w_up,
    w_down,
    qkv_b,
    out_b,
    expert_in,
    expert_out,
):
    experts = lax.axis_size("expert") * EXP_DEV
    capacity = (2 * ROWS + experts - 1) // experts + 1
    owners = lax.axis_size("dp") * lax.axis_size("expert")
    shards = (
        gain_attn_a,
        gain_mlp,
        gain_attn_b,
        gain_moe,
        bias_a,
        bias_b,
        qkv_a,
        out_a,
        w_gate,
        w_up,
        w_down,
        qkv_b,
        out_b,
    )
    small_totals = None
    pair_lists = [[] for index in range(7)]
    grad_first = jnp.zeros(expert_in.shape, jnp.float32)
    grad_second = jnp.zeros(expert_out.shape, jnp.float32)
    results = []
    grad_parts = []
    for batch in range(MICRO):
        lower = batch * ROWS
        rows = tokens[lower : lower + ROWS].astype(jnp.float32)
        grad = cotangent[lower : lower + ROWS].astype(jnp.float32)
        ids = expert_ids[lower : lower + ROWS]
        mix = jax.nn.softmax(gate_logits[lower : lower + ROWS], axis=-1)
        full = (
            lax.all_gather(shards[0], ("dp", "expert"), axis=0, tiled=True),
            lax.all_gather(shards[1], ("dp", "expert"), axis=0, tiled=True),
            lax.all_gather(shards[2], ("dp", "expert"), axis=0, tiled=True),
            lax.all_gather(shards[3], ("dp", "expert"), axis=0, tiled=True),
            lax.all_gather(shards[4], ("dp", "expert"), axis=0, tiled=True),
            lax.all_gather(shards[5], ("dp", "expert"), axis=0, tiled=True),
            lax.all_gather(shards[6], ("dp", "expert"), axis=0, tiled=True),
            lax.all_gather(shards[7], ("dp", "expert"), axis=0, tiled=True),
            lax.all_gather(shards[8], ("dp", "expert"), axis=0, tiled=True),
            lax.all_gather(shards[9], ("dp", "expert"), axis=0, tiled=True),
            lax.all_gather(shards[10], ("dp", "expert"), axis=0, tiled=True),
            lax.all_gather(shards[11], ("dp", "expert"), axis=0, tiled=True),
            lax.all_gather(shards[12], ("dp", "expert"), axis=0, tiled=True),
        )
        gains = [item.astype(jnp.float32) for item in full[0:4]]
        bias_one = full[4].astype(jnp.float32).reshape(HEADS, BUCKETS)
        bias_two = full[5].astype(jnp.float32).reshape(HEADS, BUCKETS)
        allowed, table = layout(doc_ids[batch])
        attn_one, kept_one = attention_forward(
            rows, gains[0], bias_one, full[6], full[7], allowed, table
        )
        first = rows + attn_one
        ffn, kept_ffn = feed_forward(first, gains[1], full[8], full[9], full[10])
        middle = first + ffn
        attn_two, kept_two = attention_forward(
            middle, gains[2], bias_two, full[11], full[12], allowed, table
        )
        second = middle + attn_two
        route = route_table(ids, experts, capacity)
        normed_full, scale_moe = normalize(second, gains[3])
        normed = normed_full.astype(jnp.bfloat16)
        doubled = jnp.repeat(normed, 2, axis=0)
        send = product_left(route, doubled).astype(jnp.bfloat16).reshape(capacity, experts, D)
        arrived = lax.all_to_all(send, "expert", split_axis=1, concat_axis=0, tiled=True)
        slot_all = lax.all_gather(arrived, "dp", axis=0, tiled=True)
        pre = jnp.einsum("red,edf->ref", slot_all, expert_in, preferred_element_type=jnp.float32)
        act = jax.nn.gelu(pre, approximate=False).astype(jnp.bfloat16)
        term = jnp.einsum("ref,efd->red", act, expert_out, preferred_element_type=jnp.float32)
        summed = lax.psum_scatter(term.astype(jnp.bfloat16), "dp", scatter_dimension=0, tiled=True)
        returned = lax.all_to_all(summed, "expert", split_axis=0, concat_axis=1, tiled=True)
        per_route = product(route, returned.reshape(capacity * experts, D)).reshape(ROWS, 2, D)
        moe = jnp.sum(per_route * mix[:, :, None], axis=1)
        results.append((second + moe).astype(jnp.bfloat16))
        full = (
            lax.all_gather(shards[0], ("dp", "expert"), axis=0, tiled=True),
            lax.all_gather(shards[1], ("dp", "expert"), axis=0, tiled=True),
            lax.all_gather(shards[2], ("dp", "expert"), axis=0, tiled=True),
            lax.all_gather(shards[3], ("dp", "expert"), axis=0, tiled=True),
            lax.all_gather(shards[4], ("dp", "expert"), axis=0, tiled=True),
            lax.all_gather(shards[5], ("dp", "expert"), axis=0, tiled=True),
            lax.all_gather(shards[6], ("dp", "expert"), axis=0, tiled=True),
            lax.all_gather(shards[7], ("dp", "expert"), axis=0, tiled=True),
            lax.all_gather(shards[8], ("dp", "expert"), axis=0, tiled=True),
            lax.all_gather(shards[9], ("dp", "expert"), axis=0, tiled=True),
            lax.all_gather(shards[10], ("dp", "expert"), axis=0, tiled=True),
            lax.all_gather(shards[11], ("dp", "expert"), axis=0, tiled=True),
            lax.all_gather(shards[12], ("dp", "expert"), axis=0, tiled=True),
        )
        gains = [item.astype(jnp.float32) for item in full[0:4]]
        bias_one = full[4].astype(jnp.float32).reshape(HEADS, BUCKETS)
        bias_two = full[5].astype(jnp.float32).reshape(HEADS, BUCKETS)
        grad_route = (grad[:, None, :] * mix[:, :, None]).reshape(2 * ROWS, D)
        grad_slots = lax.dot_general(
            route.astype(jnp.float32), grad_route, (((0,), (0,)), ((), ())), precision=HIGH
        )
        grad_slots = grad_slots.astype(jnp.bfloat16).reshape(capacity, experts, D)
        grad_arrived = lax.all_to_all(grad_slots, "expert", split_axis=1, concat_axis=0, tiled=True)
        grad_all = lax.all_gather(grad_arrived, "dp", axis=0, tiled=True)
        grad_second = grad_second + jnp.einsum(
            "ref,red->efd", act, grad_all, preferred_element_type=jnp.float32
        )
        grad_act = jnp.einsum(
            "red,efd->ref", grad_all, expert_out, preferred_element_type=jnp.float32
        )
        grad_pre = (grad_act * gelu_slope(pre)).astype(jnp.bfloat16)
        grad_first = grad_first + jnp.einsum(
            "red,ref->edf", slot_all, grad_pre, preferred_element_type=jnp.float32
        )
        grad_term = jnp.einsum(
            "ref,edf->red", grad_pre, expert_in, preferred_element_type=jnp.float32
        )
        grad_mine = lax.psum_scatter(grad_term, "dp", scatter_dimension=0, tiled=True).astype(
            jnp.bfloat16
        )
        grad_sent = lax.all_to_all(grad_mine, "expert", split_axis=0, concat_axis=1, tiled=True)
        grad_doubled = product(route, grad_sent.reshape(capacity * experts, D)).reshape(ROWS, 2, D)
        grad_normed = jnp.sum(grad_doubled, axis=1)
        grad_norm_rows, grad_gain_moe = norm_back(grad_normed, second, scale_moe, gains[3])
        grad_second_rows = grad + grad_norm_rows
        back_two, grads_two = attention_back(
            grad_second_rows,
            middle,
            gains[2],
            bias_two,
            full[11],
            full[12],
            allowed,
            table,
            kept_two,
        )
        grad_middle = grad_second_rows + back_two
        back_ffn, grads_ffn = feed_back(
            grad_middle, first, gains[1], full[8], full[9], full[10], kept_ffn
        )
        grad_first_rows = grad_middle + back_ffn
        back_one, grads_one = attention_back(
            grad_first_rows, rows, gains[0], bias_one, full[6], full[7], allowed, table, kept_one
        )
        grad_parts.append(grad_first_rows + back_one)
        smalls = (
            grads_one[0],
            grads_ffn[0],
            grads_two[0],
            grad_gain_moe,
            grads_one[1],
            grads_two[1],
        )
        if small_totals is None:
            small_totals = smalls
        else:
            small_totals = tuple((left + right for left, right in zip(small_totals, smalls)))
        pieces = (
            grads_one[2],
            grads_one[3],
            grads_ffn[1],
            grads_ffn[2],
            grads_ffn[3],
            grads_two[2],
            grads_two[3],
        )
        for index in range(7):
            pair_lists[index].append(pieces[index])
    matrices = tuple((weight_grad(pairs) for pairs in pair_lists))
    totals = small_totals + matrices
    split = tuple(
        (item.reshape((owners, item.shape[0] // owners) + item.shape[1:]) for item in totals)
    )
    received = jax.tree.map(
        lambda part, own: part.astype(own.dtype),
        lax.all_to_all(
            for_sending(split), ("dp", "expert"), split_axis=0, concat_axis=0, tiled=True
        ),
        split,
    )
    sums = tuple((jnp.sum(item, axis=0) for item in received))
    return (
        (jnp.concatenate(results, axis=0), jnp.concatenate(grad_parts, axis=0))
        + tuple(sums)
        + (grad_first, grad_second)
    )


def solution(mesh):
    placed = (
        P(("dp", "expert"), None),
        P(("dp", "expert"), None),
        P(("dp", "expert"), None),
        P(("dp", "expert"), None),
        P(("dp", "expert"), None),
        P(("dp", "expert")),
        P(("dp", "expert")),
        P(("dp", "expert")),
        P(("dp", "expert")),
        P(("dp", "expert")),
        P(("dp", "expert")),
        P(("dp", "expert"), None),
        P(("dp", "expert"), None),
        P(("dp", "expert"), None),
        P(("dp", "expert"), None),
        P(("dp", "expert"), None),
        P(("dp", "expert"), None),
        P(("dp", "expert"), None),
        P("expert", None, "dp"),
        P("expert", "dp", None),
    )
    return jax.shard_map(
        body,
        mesh=mesh,
        in_specs=placed,
        out_specs=(
            P(("dp", "expert"), None),
            P(("dp", "expert"), None),
            P(("dp", "expert")),
            P(("dp", "expert")),
            P(("dp", "expert")),
            P(("dp", "expert")),
            P(("dp", "expert")),
            P(("dp", "expert")),
            P(("dp", "expert"), None),
            P(("dp", "expert"), None),
            P(("dp", "expert"), None),
            P(("dp", "expert"), None),
            P(("dp", "expert"), None),
            P(("dp", "expert"), None),
            P(("dp", "expert"), None),
            P("expert", None, "dp"),
            P("expert", "dp", None),
        ),
        check_vma=False,
    )
```

profile of v0, /device:TPU:0, one launch (start us, length us, event | category | flops | bytes accessed | tf_op | source)
XLA Modules:
  0.0 1430.5 jit_solution(7629579408634838494)
XLA Ops:
  19.1 7.4 all-to-all-start.4
  28.8 41.5 %all-reduce.6 = (bf16[768]{0:T(1024)(128)(2,1)S(1)}, bf16[384]{0:T(512)(128)(2,1)S(1)}, bf16[768]{0:T(1024)(128)(2,1)S(1)}, bf16[768]{0:T(1024)(128)(2,1)S(1)}, ...) all-reduce(bf16[768]{0:T(1024)(128)(2,1)S(1)} %dynamic-update-slice, ...), channel_id=1, replica_groups=mesh['dp'=4,'expert'=8] {'dp','expert'}, use_global_device_ids=true, to_apply=%add | all-reduce | flops 3840 | bytes 15360
  86.3 45.0 %all-gather.10.cloned.1.call-done = bf16[768,768]{1,0:T(8,128)(2,1)} async-done(((bf16[24,768]{1,0:T(8,128)(2,1)}), bf16[768,768]{1,0:T(8,128)(2,1)}) %all-gather.10.cloned.1.call-update) | async-done | bytes 1179664 | tf_op jit(solution)/shard_map/all_gather | solution.py:237
  147.7 49.1 %all-gather.12.cloned.1.call-done = bf16[768,3072]{1,0:T(8,128)(2,1)} async-done(((bf16[24,3072]{1,0:T(8,128)(2,1)}), bf16[768,3072]{1,0:T(8,128)(2,1)}) %all-gather.12.cloned.1.call-update) | async-done | bytes 4718608 | tf_op jit(solution)/shard_map/all_gather | solution.py:238
  196.8 4.2 fusion.257
  201.1 61.1 %all-gather.14.cloned.1.call-done = bf16[768,3072]{1,0:T(8,128)(2,1)} async-done(((bf16[24,3072]{1,0:T(8,128)(2,1)}), bf16[768,3072]{1,0:T(8,128)(2,1)}) %all-gather.14.cloned.1.call-update) | async-done | bytes 4718608 | tf_op jit(solution)/shard_map/all_gather | solution.py:239
  262.1 6.1 multiply_convert_fusion.3
  268.2 59.1 %all-gather.16.cloned.1.call-done = bf16[3072,768]{1,0:T(8,128)(2,1)} async-done(((bf16[96,768]{1,0:T(8,128)(2,1)}), bf16[3072,768]{1,0:T(8,128)(2,1)}) %all-gather.16.cloned.1.call-update) | async-done | bytes 4718608 | tf_op jit(solution)/shard_map/all_gather | solution.py:240
  327.4 3.5 multiply_reduce_fusion.20
  332.3 56.9 %all-gather.18.cloned.1.call-done = bf16[768,2304]{1,0:T(8,128)(2,1)} async-done(((bf16[24,2304]{1,0:T(8,128)(2,1)}), bf16[768,2304]{1,0:T(8,128)(2,1)}) %all-gather.18.cloned.1.call-update) | async-done | bytes 3538960 | tf_op jit(solution)/shard_map/all_gather | solution.py:241
  389.2 3.5 convolution_convert_fusion.7
  403.5 41.6 %all-gather.20.cloned.1.call-done = bf16[768,768]{1,0:T(8,128)(2,1)} async-done(((bf16[24,768]{1,0:T(8,128)(2,1)}), bf16[768,768]{1,0:T(8,128)(2,1)}) %all-gather.20.cloned.1.call-update) | async-done | bytes 1179664 | tf_op jit(solution)/shard_map/all_gather | solution.py:242
  452.7 4.4 all-to-all-start
  458.3 9.9 all_gather.49
  470.5 9.6 all_gather.47
  480.1 8.0 fusion.2
  510.4 6.3 multiply_convert_fusion.2
  516.6 8.2 reduce-scatter.9.cloned.1.call-done
  526.7 5.7 all-to-all-start.5
  532.5 4.1 multiply_reduce_fusion.17
  537.2 4.0 all-to-all-done.5
  561.7 4.8 multiply_reduce_fusion.7
  583.4 4.1 all-to-all-start.2
  594.3 3.6 fusion.46
  600.2 8.7 all_gather.48
  613.2 7.2 fusion.47
  623.2 18.5 %all_to_all.203 = bf16[5,32,768]{2,0,1:T(8,128)(2,1)S(1)} all-to-all(bf16[5,32,768]{2,0,1:T(8,128)(2,1)S(1)} %copy.379), channel_id=1, replica_groups=mesh['dp'=4,'expert'=8] {'expert'}, dimensions={1} | all-to-all | bytes 491520 | tf_op jit(solution)/shard_map/all_to_all | solution.py:296
  641.9 14.8 %all_gather.50 = bf16[160,4,768]{2,0,1:T(8,128)(2,1)S(1)} all-gather(bf16[40,4,768]{2,0,1:T(8,128)(2,1)S(1)} %copy.382), channel_id=1, replica_groups=mesh['dp'=4,'expert'=8] {'dp'}, dimensions={0}, use_global_device_ids=true | all-gather | bytes 1228800 | tf_op jit(solution)/shard_map/all_gather | solution.py:297
  656.7 4.5 fusion.17
  667.0 4.0 all-to-all-start.1
  672.9 7.6 all-to-all-done.1
  680.6 4.0 all-to-all-start.3
  695.9 6.3 all-to-all-start.7
  726.9 4.0 multiply_convert_fusion.1
  732.6 5.2 multiply_reduce_fusion.9
  742.0 4.0 multiply_reduce_fusion.6
  747.5 4.6 multiply_convert_fusion
  786.8 5.2 all-to-all-start.12
  799.0 4.8 all-to-all-start.13
  805.3 5.6 all-to-all-done.13
  814.9 5.6 all-to-all-done.8
  824.5 5.6 all-to-all-done.9
  833.4 6.3 all-to-all-done.10
  845.0 4.3 all-to-all-done.11
  854.2 28.8 %all-to-all-done.15 = bf16[32,24,768]{2,1,0:T(8,128)(2,1)S(1)} async-done(((bf16[32,24,768]{2,1,0:T(8,128)(2,1)}), bf16[32,24,768]{2,1,0:T(8,128)(2,1)S(1)}, u32[]{:S(2)}, u32[]{:S(2)}) %all-to-all-start.15) | async-done | bytes 1179680 | tf_op jit(solution)/shard_map/all_to_all | solution.py:369
  888.6 27.4 %all-to-all-done.20 = bf16[32,24,768]{2,1,0:T(8,128)(2,1)S(1)} async-done(((bf16[32,24,768]{2,1,0:T(8,128)(2,1)}), bf16[32,24,768]{2,1,0:T(8,128)(2,1)S(1)}, u32[]{:S(2)}, u32[]{:S(2)}) %all-to-all-start.20) | async-done | bytes 1179680 | tf_op jit(solution)/shard_map/all_to_all | solution.py:369
  919.8 4.1 convolution_convert_fusion
  923.9 77.5 %all-to-all-done.14 = bf16[32,24,2304]{2,1,0:T(8,128)(2,1)S(1)} async-done(((bf16[32,24,2304]{2,1,0:T(8,128)(2,1)}), bf16[32,24,2304]{2,1,0:T(8,128)(2,1)S(1)}, u32[]{:S(2)}, u32[]{:S(2)}) %all-to-all-start.14) | async-done | bytes 3538976 | tf_op jit(solution)/shard_map/all_to_all | solution.py:369
  1001.4 3.6 all-to-all-start.19
  1005.0 4.8 convolution_convert_fusion.3
  1009.8 76.8 %all-to-all-done.19 = bf16[32,24,2304]{2,1,0:T(8,128)(2,1)} async-done(((bf16[32,24,2304]{2,1,0:T(8,128)(2,1)}), bf16[32,24,2304]{2,1,0:T(8,128)(2,1)}, u32[]{:S(2)}, u32[]{:S(2)}) %all-to-all-start.19) | async-done | bytes 3538976 | tf_op jit(solution)/shard_map/all_to_all | solution.py:369
  1086.6 3.6 all-to-all-start.16
  1090.2 4.8 convolution_convert_fusion.2
  1095.0 102.7 %all-to-all-done.16 = bf16[32,24,3072]{2,1,0:T(8,128)(2,1)} async-done(((bf16[32,24,3072]{2,1,0:T(8,128)(2,1)}), bf16[32,24,3072]{2,1,0:T(8,128)(2,1)}, u32[]{:S(2)}, u32[]{:S(2)}) %all-to-all-start.16) | async-done | bytes 4718624 | tf_op jit(solution)/shard_map/all_to_all | solution.py:369
  1197.7 3.6 all-to-all-start.17
  1201.3 4.8 convolution_convert_fusion.1
  1206.1 102.7 %all-to-all-done.17 = bf16[32,24,3072]{2,1,0:T(8,128)(2,1)} async-done(((bf16[32,24,3072]{2,1,0:T(8,128)(2,1)}), bf16[32,24,3072]{2,1,0:T(8,128)(2,1)}, u32[]{:S(2)}, u32[]{:S(2)}) %all-to-all-start.17) | async-done | bytes 4718624 | tf_op jit(solution)/shard_map/all_to_all | solution.py:369
  1308.8 3.8 all-to-all-start.18
  1317.3 5.3 convolution_add_fusion.1
  1322.7 7.6 convolution_add_fusion
  1342.2 4.0 convert_reduce_fusion.2
  1346.2 4.0 convert_reduce_fusion.1
  1350.2 69.8 %all-to-all-done.18 = bf16[32,96,768]{2,1,0:T(8,128)(2,1)} async-done(((bf16[32,96,768]{2,1,0:T(8,128)(2,1)}), bf16[32,96,768]{2,1,0:T(8,128)(2,1)}, u32[]{:S(2)}, u32[]{:S(2)}) %all-to-all-start.18) | async-done | bytes 4718624 | tf_op jit(solution)/shard_map/all_to_all | solution.py:369
  1420.0 3.7 convert_reduce_fusion
  (627 shorter events, 287.7 us)
Async XLA Ops:
  7.2 69.3 %all-gather.8.cloned.1.call-start = ((), (), s32[]{:S(2)}) async-start(), calls=%async_computation.25 | async-start | bytes 3649536 | tf_op jit(solution)/shard_map/all_gather | solution.py:236
  7.9 123.4 %all-gather.10.cloned.1.call-start = ((), (), s32[]{:S(2)}) async-start(), calls=%async_computation.26 | async-start | bytes 1216512 | tf_op jit(solution)/shard_map/all_gather | solution.py:237
  8.7 188.2 %all-gather.12.cloned.1.call-start = ((), (), s32[]{:S(2)}) async-start(), calls=%async_computation.27 | async-start | bytes 4866048 | tf_op jit(solution)/shard_map/all_gather | solution.py:238
  9.4 252.7 %all-gather.14.cloned.1.call-start = ((), (), s32[]{:S(2)}) async-start(), calls=%async_computation.28 | async-start | bytes 4866048 | tf_op jit(solution)/shard_map/all_gather | solution.py:239
  10.0 317.4 %all-gather.16.cloned.1.call-start = ((), (), s32[]{:S(2)}) async-start(), calls=%async_computation.29 | async-start | bytes 4866048 | tf_op jit(solution)/shard_map/all_gather | solution.py:240
  10.6 378.6 %all-gather.18.cloned.1.call-start = ((), (), s32[]{:S(2)}) async-start(), calls=%async_computation.30 | async-start | bytes 3649536 | tf_op jit(solution)/shard_map/all_gather | solution.py:241
  14.9 12.4 copy-start.151
  14.9 12.7 copy-start.152
  14.9 12.9 copy-start.153
  14.9 13.1 copy-start.154
  14.9 13.4 copy-start.155
  15.0 13.6 copy-start.156
  15.0 55.3 %copy-start.30 = (bf16[128,768]{1,0:T(8,128)(2,1)S(1)}, bf16[128,768]{1,0:T(8,128)(2,1)}, u32[]{:S(2)}) copy-start(bf16[128,768]{1,0:T(8,128)(2,1)} %param.20) | copy-start | bytes 589828
  17.8 53.0 %copy-start.142 = (s32[128]{0:T(128)}, s32[128]{0:T(128)S(1)}, u32[]{:S(2)}) copy-start(s32[128]{0:T(128)S(1)} %get-tuple-element.96) | copy-start | bytes 1540
  19.1 54.1 %copy-start.147 = (s32[2,64]{1,0:T(2,128)S(1)}, s32[2,64]{1,0:T(2,128)}, u32[]{:S(2)}) copy-start(s32[2,64]{1,0:T(2,128)} %param.22) | copy-start | bytes 1540
  19.1 433.6 %all-to-all-start.4 = ((bf16[5,32,768]{2,0,1:T(8,128)(2,1)}), bf16[5,32,768]{2,0,1:T(8,128)(2,1)}, u32[]{:S(2)}, u32[]{:S(2)}) async-start(bf16[5,32,768]{2,0,1:T(8,128)(2,1)} %copy.348), calls=%async_computation.4 | async-start | bytes 786432 | tf_op jit(solution)/shard_map/all_to_all | solution.py:296
  26.5 418.6 %all-gather.20.cloned.1.call-start = ((), (), s32[]{:S(2)}) async-start(), calls=%async_computation.31 | async-start | bytes 1216512 | tf_op jit(solution)/shard_map/all_gather | solution.py:242
  27.3 43.2 %copy-start.106 = (s32[64,64]{0,1:T(8,128)}, s32[64,64]{0,1:T(8,128)S(1)}, u32[]{:S(2)}) copy-start(s32[64,64]{0,1:T(8,128)S(1)} %fusion.222) | copy-start | bytes 49156
  82.2 52.1 %copy-start = (bf16[768,2304]{1,0:T(8,128)(2,1)S(1)}, bf16[768,2304]{1,0:T(8,128)(2,1)}, u32[]{:S(2)}) copy-start(bf16[768,2304]{1,0:T(8,128)(2,1)} %all-gather.8.cloned.1.call-done) | copy-start | bytes 10616836
  452.7 16.6 %all-to-all-start = ((bf16[5,32,768]{2,0,1:T(8,128)(2,1)}), bf16[5,32,768]{2,0,1:T(8,128)(2,1)}, u32[]{:S(2)}, u32[]{:S(2)}) async-start(bf16[5,32,768]{2,0,1:T(8,128)(2,1)} %copy.323), calls=%async_computation | async-start | bytes 786432 | tf_op jit(solution)/shard_map/all_to_all | solution.py:263
  457.1 67.8 %reduce-scatter.9.cloned.1.call-start = ((), (), s32[]{:S(2)}) async-start(), calls=%async_computation.32 | async-start | bytes 2457600 | tf_op jit(solution)/shard_map/reduce_scatter | solution.py:311
  470.4 17.6 %slice-start.10 = ((s8[4718592]{0:T(1024)(128)(4,1)}), s8[4194304]{0:T(1024)(128)(4,1)S(1)}, s32[]{:S(2)}) async-start(s8[4718592]{0:T(1024)(128)(4,1)} %bitcast.442), calls=%async_computation.46 | async-start | bytes 8388608
  470.4 20.6 %slice-start.4 = ((s8[4718592]{0:T(1024)(128)(4,1)}), s8[4194304]{0:T(1024)(128)(4,1)S(1)}, s32[]{:S(2)}) async-start(s8[4718592]{0:T(1024)(128)(4,1)} %bitcast.433), calls=%async_computation.40 | async-start | bytes 8388608
  480.1 10.9 slice-start.5
  526.7 14.4 %all-to-all-start.5 = ((bf16[40,4,768]{2,1,0:T(4,128)(2,1)}), bf16[40,4,768]{2,1,0:T(4,128)(2,1)}, u32[]{:S(2)}, u32[]{:S(2)}) async-start(bf16[40,4,768]{2,1,0:T(4,128)(2,1)} %copy.352), calls=%async_computation.6 | async-start | bytes 491520 | tf_op jit(solution)/shard_map/all_to_all | solution.py:314
  583.4 15.6 %all-to-all-start.2 = ((bf16[5,32,768]{2,0,1:T(8,128)(2,1)}), bf16[5,32,768]{2,0,1:T(8,128)(2,1)}, u32[]{:S(2)}, u32[]{:S(2)}) async-start(bf16[5,32,768]{2,0,1:T(8,128)(2,1)} %copy.341), calls=%async_computation.2 | async-start | bytes 786432 | tf_op jit(solution)/shard_map/all_to_all | solution.py:263
  587.5 77.6 %reduce-scatter.13.cloned.1.call-start = ((), (), s32[]{:S(2)}) async-start(), calls=%async_computation.34 | async-start | bytes 1228800
  599.0 72.1 %reduce-scatter.15.cloned.1.call-start = ((), (), s32[]{:S(2)}) async-start(), calls=%async_computation.35 | async-start | bytes 1228800
  621.5 72.5 %reduce-scatter.11.cloned.1.call-start = ((), (), s32[]{:S(2)}) async-start(), calls=%async_computation.33 | async-start | bytes 2457600 | tf_op jit(solution)/shard_map/reduce_scatter | solution.py:311
  623.0 33.7 %copy-start.53 = (f32[4,160,768]{2,1,0:T(8,128)S(1)}, f32[4,160,768]{2,1,0:T(8,128)}, u32[]{:S(2)}) copy-start(f32[4,160,768]{2,1,0:T(8,128)} %copy-done.52) | copy-start | bytes 5898244
  623.1 39.1 %slice-start.6 = ((s8[4718592]{0:T(1024)(128)(4,1)}), s8[4194304]{0:T(1024)(128)(4,1)S(1)}, s32[]{:S(2)}) async-start(s8[4718592]{0:T(1024)(128)(4,1)} %bitcast.435), calls=%async_computation.42 | async-start | bytes 8388608
  667.0 13.5 all-to-all-start.1
  680.6 15.3 %all-to-all-start.3 = ((bf16[40,4,768]{2,1,0:T(4,128)(2,1)}), bf16[40,4,768]{2,1,0:T(4,128)(2,1)}, u32[]{:S(2)}, u32[]{:S(2)}) async-start(bf16[40,4,768]{2,1,0:T(4,128)(2,1)} %reshape.712), calls=%async_computation.3 | async-start | bytes 491520 | tf_op jit(solution)/shard_map/all_to_all | solution.py:269
  695.9 14.7 %all-to-all-start.7 = ((bf16[40,4,768]{2,1,0:T(4,128)(2,1)}), bf16[40,4,768]{2,1,0:T(4,128)(2,1)}, u32[]{:S(2)}, u32[]{:S(2)}) async-start(bf16[40,4,768]{2,1,0:T(4,128)(2,1)} %copy.383), calls=%async_computation.9 | async-start | bytes 491520 | tf_op jit(solution)/shard_map/all_to_all | solution.py:314
  742.0 10.1 slice-start.2
  742.0 11.8 slice-start.8
  786.8 12.2 all-to-all-start.12
  794.4 28.7 %copy-start.128 = (f32[768]{0:T(1024)S(1)}, f32[768]{0:T(1024)}, u32[]{:S(2)}) copy-start(f32[768]{0:T(1024)} %get-tuple-element.21) | copy-start | bytes 9220
  794.4 38.3 %copy-start.126 = (f32[768]{0:T(1024)S(1)}, f32[768]{0:T(1024)}, u32[]{:S(2)}) copy-start(f32[768]{0:T(1024)} %get-tuple-element.19) | copy-start | bytes 9220
  794.4 38.3 %copy-start.127 = (f32[768]{0:T(1024)S(1)}, f32[768]{0:T(1024)}, u32[]{:S(2)}) copy-start(f32[768]{0:T(1024)} %get-tuple-element.17) | copy-start | bytes 9220
  799.0 11.9 all-to-all-start.13
  810.9 38.4 %copy-start.115 = (bf16[32,1,12]{2,1,0:T(2,128)(2,1)}, bf16[32,1,12]{2,1,0:T(2,128)(2,1)S(1)}, u32[]{:S(2)}) copy-start(bf16[32,1,12]{2,1,0:T(2,128)(2,1)S(1)} %all-to-all-done.13) | copy-start | bytes 2308
  810.9 9.6 all-to-all-start.8
  820.5 28.8 %copy-start.117 = (bf16[32,1,24]{2,1,0:T(2,128)(2,1)}, bf16[32,1,24]{2,1,0:T(2,128)(2,1)S(1)}, u32[]{:S(2)}) copy-start(bf16[32,1,24]{2,1,0:T(2,128)(2,1)S(1)} %all-to-all-done.8) | copy-start | bytes 4612
  820.5 9.6 all-to-all-start.9
  830.1 19.2 %copy-start.119 = (bf16[32,1,24]{2,1,0:T(2,128)(2,1)}, bf16[32,1,24]{2,1,0:T(2,128)(2,1)S(1)}, u32[]{:S(2)}) copy-start(bf16[32,1,24]{2,1,0:T(2,128)(2,1)S(1)} %all-to-all-done.9) | copy-start | bytes 4612
  830.1 9.6 all-to-all-start.10
  839.7 9.6 copy-start.121
  839.7 9.6 all-to-all-start.11
  842.3 10.3 copy-start.58
  842.3 10.3 copy-start.60
  842.3 10.3 copy-start.79
  842.3 10.3 copy-start.81
  849.9 33.1 %all-to-all-start.15 = ((bf16[32,24,768]{2,1,0:T(8,128)(2,1)}), bf16[32,24,768]{2,1,0:T(8,128)(2,1)S(1)}, u32[]{:S(2)}, u32[]{:S(2)}) async-start(bf16[32,24,768]{2,1,0:T(8,128)(2,1)} %bitcast.91), calls=%async_computation.17 | async-start | bytes 2359296 | tf_op jit(solution)/shard_map/all_to_all | solution.py:369
  852.6 33.0 %copy-start.50 = (bf16[64,2304]{1,0:T(8,128)(2,1)S(1)}, bf16[64,2304]{1,0:T(8,128)(2,1)}, u32[]{:S(2)}) copy-start(bf16[64,2304]{1,0:T(8,128)(2,1)} %convert_element_type.499) | copy-start | bytes 884740
  852.6 33.0 %copy-start.51 = (bf16[64,2304]{1,0:T(8,128)(2,1)S(1)}, bf16[64,2304]{1,0:T(8,128)(2,1)}, u32[]{:S(2)}) copy-start(bf16[64,2304]{1,0:T(8,128)(2,1)} %convert_element_type.514) | copy-start | bytes 884740
  854.2 31.5 %copy-start.85 = (bf16[64,768]{1,0:T(8,128)(2,1)S(1)}, bf16[64,768]{1,0:T(8,128)(2,1)}, u32[]{:S(2)}) copy-start(bf16[64,768]{1,0:T(8,128)(2,1)} %copy-done.84) | copy-start | bytes 294916
  854.2 31.5 %copy-start.86 = (bf16[64,768]{1,0:T(8,128)(2,1)S(1)}, bf16[64,768]{1,0:T(8,128)(2,1)}, u32[]{:S(2)}) copy-start(bf16[64,768]{1,0:T(8,128)(2,1)} %get-tuple-element.79) | copy-start | bytes 294916
  883.0 33.1 %all-to-all-start.20 = ((bf16[32,24,768]{2,1,0:T(8,128)(2,1)}), bf16[32,24,768]{2,1,0:T(8,128)(2,1)S(1)}, u32[]{:S(2)}, u32[]{:S(2)}) async-start(bf16[32,24,768]{2,1,0:T(8,128)(2,1)} %bitcast.98), calls=%async_computation.22 | async-start | bytes 2359296 | tf_op jit(solution)/shard_map/all_to_all | solution.py:369
  917.0 84.4 %all-to-all-start.14 = ((bf16[32,24,2304]{2,1,0:T(8,128)(2,1)}), bf16[32,24,2304]{2,1,0:T(8,128)(2,1)S(1)}, u32[]{:S(2)}, u32[]{:S(2)}) async-start(bf16[32,24,2304]{2,1,0:T(8,128)(2,1)} %bitcast.88), calls=%async_computation.16 | async-start | bytes 7077888 | tf_op jit(solution)/shard_map/all_to_all | solution.py:369
  1001.4 85.2 %all-to-all-start.19 = ((bf16[32,24,2304]{2,1,0:T(8,128)(2,1)}), bf16[32,24,2304]{2,1,0:T(8,128)(2,1)}, u32[]{:S(2)}, u32[]{:S(2)}) async-start(bf16[32,24,2304]{2,1,0:T(8,128)(2,1)} %bitcast.95), calls=%async_computation.21 | async-start | bytes 7077888 | tf_op jit(solution)/shard_map/all_to_all | solution.py:369
  1086.6 111.1 %all-to-all-start.16 = ((bf16[32,24,3072]{2,1,0:T(8,128)(2,1)}), bf16[32,24,3072]{2,1,0:T(8,128)(2,1)}, u32[]{:S(2)}, u32[]{:S(2)}) async-start(bf16[32,24,3072]{2,1,0:T(8,128)(2,1)} %bitcast.439), calls=%async_computation.18 | async-start | bytes 9437184 | tf_op jit(solution)/shard_map/all_to_all | solution.py:369
  1197.7 111.1 %all-to-all-start.17 = ((bf16[32,24,3072]{2,1,0:T(8,128)(2,1)}), bf16[32,24,3072]{2,1,0:T(8,128)(2,1)}, u32[]{:S(2)}, u32[]{:S(2)}) async-start(bf16[32,24,3072]{2,1,0:T(8,128)(2,1)} %bitcast.438), calls=%async_computation.19 | async-start | bytes 9437184 | tf_op jit(solution)/shard_map/all_to_all | solution.py:369
  1308.8 111.2 %all-to-all-start.18 = ((bf16[32,96,768]{2,1,0:T(8,128)(2,1)}), bf16[32,96,768]{2,1,0:T(8,128)(2,1)}, u32[]{:S(2)}, u32[]{:S(2)}) async-start(bf16[32,96,768]{2,1,0:T(8,128)(2,1)} %bitcast.437), calls=%async_computation.20 | async-start | bytes 9437184 | tf_op jit(solution)/shard_map/all_to_all | solution.py:369
  (137 other events, 461.5 us)
Sparse Core Ops, SparseCore 0:
  10.9 64.3 all-gather.7
  78.3 53.0 all-gather.9
  134.3 62.5 all-gather.11
  199.6 62.4 all-gather.13
  264.9 62.4 all-gather.15
  330.2 58.9 all-gather.17
  392.1 52.9 all-gather.19
  494.1 30.7 reduce-scatter.8
  599.1 24.8 reduce-scatter.12
  627.0 29.6 reduce-scatter.14
  665.3 28.3 reduce-scatter.10
where the time goes:
time: 1440 us; the launch traced here: 1430 us
  waiting for transfers between devices  853 us (59%)
  matrix products  205 us (14%)
  local copies, waits for them, and re-layouts  116 us (8%)
  blocking collectives  103 us (7%)
  starting transfers between devices  79.2 us (6%)
  other arithmetic  58.1 us (4%)
  between operations  16.5 us (1%)
    all_to_all x13, waiting for transfers between devices, body(): lax.all_to_all(for_sending(split), ('dp', 'expert'), split_axis=0, concat...  514 us
    all_gather x1, waiting for transfers between devices, body(): lax.all_gather(shards[9], ('dp', 'expert'), axis=0, tiled=True)  61.1 us
    all_gather x1, waiting for transfers between devices, body(): lax.all_gather(shards[10], ('dp', 'expert'), axis=0, tiled=True)  59.1 us
    all_gather x1, waiting for transfers between devices, body(): lax.all_gather(shards[11], ('dp', 'expert'), axis=0, tiled=True)  56.9 us
    dot_general x18, matrix products, product(): return jnp.dot(left, right, preferred_element_type=jnp.float32)  49.5 us
    all_gather x1, waiting for transfers between devices, body(): lax.all_gather(shards[8], ('dp', 'expert'), axis=0, tiled=True)  49.1 us
    all_gather x1, waiting for transfers between devices, body(): lax.all_gather(shards[7], ('dp', 'expert'), axis=0, tiled=True)  45 us
    all_to_all x13, starting transfers between devices, body(): lax.all_to_all(for_sending(split), ('dp', 'expert'), split_axis=0, concat...  42.8 us
  transfers between devices with their start and end apart: 31, of which 23 were waited for; matrix products, arithmetic and copies ran while one was open for 16% of the time, Pallas kernels for 0%

commit v1 on v0

v1 whole, which is shorter than its diff:
```python
import functools
import math

import jax
import jax.numpy as jnp
from jax import lax
from jax.experimental import pallas as pl
from jax.experimental.pallas import tpu as pltpu
from jax.sharding import PartitionSpec as P

D = 768
HEADS = 12
HEAD_DIM = 64
BUCKETS = 32
EXP_DEV = 4
ROWS = 64
MICRO = 2
AXES = ("dp", "expert")
MESH = pl.DeviceIdType.MESH

EPSILON = 1e-06
ROOT_HALF = 0.7071067811865476
ROOT_TWO_PI = 0.3989422804014327
FACTOR = 1.0 / math.sqrt(HEAD_DIM)


class Cube:
    def __init__(self, dp, expert):
        self.low = expert.bit_length() - 1
        self.bits = (dp * expert).bit_length() - 1
        self.sizes = (dp, expert)
        self.core = self.bits - self.low - 1

    def coordinates(self):
        dp, expert = lax.axis_index("dp"), lax.axis_index("expert")
        out = []
        for bit in range(self.bits):
            shift = self.bits - 1 - bit
            if shift >= self.low:
                out.append(lax.rem(lax.div(dp, 1 << (shift - self.low)), 2))
            else:
                out.append(lax.rem(lax.div(expert, 1 << shift), 2))
        return out

    def partner(self, bit, here):
        dp, expert = lax.axis_index("dp"), lax.axis_index("expert")
        shift = self.bits - 1 - bit
        if shift >= self.low:
            step = 1 << (shift - self.low)
            return (dp + step - 2 * step * here[bit], expert)
        step = 1 << shift
        return (dp, expert + step - 2 * step * here[bit])

    def orders(self):
        others = [bit for bit in range(self.core)]
        inner = [bit for bit in range(self.core + 1, self.bits)]
        first = inner[:-1] + inner[-1:] + others + [self.core]
        second = inner[:-1] + others + inner[-1:] + [self.core]
        return (first, second)

    def greet(self, here):
        barrier = pltpu.get_barrier_semaphore()
        for bit in range(self.bits):
            pl.semaphore_signal(
                barrier, inc=1, device_id=self.partner(bit, here), device_id_type=MESH
            )
        pl.semaphore_wait(barrier, self.bits)


def gather_kernel(cube, count, *refs):
    sources, outs = refs[:count], refs[count : 2 * count]
    local_sem, send_sem, recv_sem = refs[2 * count :]
    here = cube.coordinates()
    orders = cube.orders()
    own = []
    for index in range(count):
        copy = pltpu.make_async_copy(
            sources[index], outs[index].at[tuple(here)], local_sem.at[index]
        )
        copy.start()
        own.append(copy)
    cube.greet(here)
    going = [None] * count
    for tick in range(cube.bits + (count - 1) // 2 + 1):
        for index in range(count):
            stage = tick - index // 2
            if not 0 <= stage <= cube.bits:
                continue
            if stage == 0:
                own[index].wait()
            else:
                going[index].wait()
            if stage == cube.bits:
                continue
            order = orders[index % 2]
            done = order[:stage]
            place = tuple(slice(None) if b in done else here[b] for b in range(cube.bits))
            block = outs[index].at[place]
            copy = pltpu.make_async_remote_copy(
                src_ref=block,
                dst_ref=block,
                send_sem=send_sem.at[index, stage],
                recv_sem=recv_sem.at[index, stage],
                device_id=cube.partner(order[stage], here),
                device_id_type=MESH,
            )
            copy.start()
            going[index] = copy


def gather_all(cube, shards):
    count = len(shards)
    lead = (2,) * cube.bits
    full = pl.pallas_call(
        functools.partial(gather_kernel, cube, count),
        out_shape=[jax.ShapeDtypeStruct(lead + s.shape, s.dtype) for s in shards],
        in_specs=[pl.BlockSpec(memory_space=pl.ANY)] * count,
        out_specs=[pl.BlockSpec(memory_space=pl.ANY)] * count,
        scratch_shapes=[
            pltpu.SemaphoreType.DMA((count,)),
            pltpu.SemaphoreType.DMA((count, cube.bits)),
            pltpu.SemaphoreType.DMA((count, cube.bits)),
        ],
        compiler_params=pltpu.CompilerParams(collective_id=0, has_side_effects=True),
    )(*shards)
    return [f.reshape((-1,) + f.shape[-1:]) for f in full]


def reduce_kernel(cube, count, *refs):
    sources, outs = refs[:count], refs[count : 2 * count]
    rest = refs[2 * count :]
    totals = rest[:count]
    slots = [
        rest[count + index * cube.bits : count + (index + 1) * cube.bits] for index in range(count)
    ]
    local_sem, send_sem, recv_sem = rest[count + count * cube.bits :]
    here = cube.coordinates()
    orders = [list(reversed(order)) for order in cube.orders()]
    core = cube.core
    own = []
    for index in range(count):
        place = tuple(here[b] if b == core else slice(None) for b in range(cube.bits))
        copy = pltpu.make_async_copy(
            sources[index].at[place], totals[index], local_sem.at[index]
        )
        copy.start()
        own.append(copy)
    cube.greet(here)
    going = [None] * count
    others = [b for b in range(cube.bits) if b != core]

    def add(index, stage):
        order = orders[index % 2]
        done = order[: stage + 1]
        live = [b for b in others if b not in done]
        slot, total = slots[index][stage], totals[index]
        if not live:
            outs[index][...] = total[tuple(here[b] for b in others)].astype(jnp.float32) + slot[
                ...
            ].astype(jnp.float32)
            return

        def step(k, carry):
            where, inner = {}, []
            for position, b in enumerate(live):
                where[b] = lax.rem(lax.div(k, 1 << (len(live) - 1 - position)), 2)
                inner.append(where[b])
            at = tuple(where[b] if b in where else here[b] for b in others)
            left = total[at].astype(jnp.float32)
            right = slot[tuple(inner)].astype(jnp.float32)
            total[at] = (left + right).astype(total.dtype)
            return carry

        lax.fori_loop(0, 1 << len(live), step, 0)

    for tick in range(cube.bits + (count - 1) // 2 + 1):
        for index in range(count):
            stage = tick - index // 2
            if not 0 <= stage <= cube.bits:
                continue
            order = orders[index % 2]
            if stage > 0:
                if stage == 1:
                    own[index].wait()
                going[index].wait()
                add(index, stage - 1)
            if stage == cube.bits:
                continue
            bit = order[stage]
            done = order[:stage]
            if stage == 0:
                place = tuple(1 - here[b] if b == bit else slice(None) for b in range(cube.bits))
                block = sources[index].at[place]
            else:
                place = tuple(
                    1 - here[b] if b == bit else (here[b] if b in done else slice(None))
                    for b in others
                )
                block = totals[index].at[place]
            copy = pltpu.make_async_remote_copy(
                src_ref=block,
                dst_ref=slots[index][stage],
                send_sem=send_sem.at[index, stage],
                recv_sem=recv_sem.at[index, stage],
                device_id=cube.partner(bit, here),
                device_id_type=MESH,
            )
            copy.start()
            going[index] = copy


def reduce_all(cube, wholes):
    count = len(wholes)
    lead = (2,) * cube.bits
    shapes = [w.shape[1:] for w in wholes]
    wholes = [w.reshape(lead + w.shape[1:]) for w in wholes]
    scratch = [
        pltpu.VMEM((2,) * (cube.bits - 1) + shape, w.dtype) for shape, w in zip(shapes, wholes)
    ]
    for shape, w in zip(shapes, wholes):
        for stage in range(cube.bits):
            scratch.append(pltpu.VMEM((2,) * (cube.bits - 1 - stage) + shape, w.dtype))
    return pl.pallas_call(
        functools.partial(reduce_kernel, cube, count),
        out_shape=[jax.ShapeDtypeStruct(shape, jnp.float32) for shape in shapes],
        in_specs=[pl.BlockSpec(memory_space=pl.ANY)] * count,
        out_specs=[pl.BlockSpec(memory_space=pltpu.VMEM)] * count,
        scratch_shapes=scratch
        + [
            pltpu.SemaphoreType.DMA((count,)),
            pltpu.SemaphoreType.DMA((count, cube.bits)),
            pltpu.SemaphoreType.DMA((count, cube.bits)),
        ],
        compiler_params=pltpu.CompilerParams(
            collective_id=1, has_side_effects=True, vmem_limit_bytes=58 * 2**20
        ),
    )(*wholes)


def product(left, right):
    return jnp.dot(left, right, preferred_element_type=jnp.float32)


def product_left(left, right):
    return lax.dot_general(
        left, right, (((0,), (0,)), ((), ())), preferred_element_type=jnp.float32
    )


def product_right(left, right):
    return lax.dot_general(
        left, right, (((1,), (1,)), ((), ())), preferred_element_type=jnp.float32
    )


def einsum(spec, left, right):
    return jnp.einsum(spec, left, right, preferred_element_type=jnp.float32)


def gelu_slope(values):
    return (
        0.5 * (1.0 + lax.erf(values * ROOT_HALF))
        + values * jnp.exp(-0.5 * values * values) * ROOT_TWO_PI
    )


def normalize(rows, gain):
    scale = lax.rsqrt(jnp.mean(rows * rows, axis=-1, keepdims=True) + EPSILON)
    return (rows * scale * gain, scale)


def norm_back(grad, rows, scale, gain):
    unit = rows * scale
    grad_gain = jnp.sum(grad * unit, axis=0)
    inner = grad * gain
    return (scale * (inner - unit * jnp.mean(inner * unit, axis=-1, keepdims=True)), grad_gain)


def layout(docs):
    place = jnp.arange(ROWS, dtype=jnp.int32)
    apart = place[:, None] - place[None, :]
    allowed = (apart >= 0)[None] & (docs[:, :, None] == docs[:, None, :])
    bucket = jnp.clip(apart, 0, BUCKETS - 1)
    table = (bucket[:, :, None] == jnp.arange(BUCKETS, dtype=jnp.int32)[None, None, :]).astype(
        jnp.bfloat16
    )
    return (allowed, table)


def score_of(queries, keys, bias, allowed, table):
    scores = einsum("mqhd,mkhd->mhqk", queries, keys) * FACTOR
    scores = scores + einsum("hb,qkb->hqk", bias, table)[None]
    return jnp.where(allowed[:, None], scores, -1000000000.0)


def attention_forward(rows, gain, bias, wqkv, wout, allowed, table):
    count = rows.shape[0]
    normed_full, scale = normalize(rows, gain)
    normed = normed_full.astype(jnp.bfloat16)
    mixed = product(normed, wqkv).astype(jnp.bfloat16).reshape(-1, ROWS, 3, HEADS, HEAD_DIM)
    queries, keys, values = (mixed[:, :, 0], mixed[:, :, 1], mixed[:, :, 2])
    scores = score_of(queries, keys, bias, allowed, table)
    top = jnp.max(scores, axis=-1, keepdims=True)
    raised = jnp.exp(scores - top)
    attend = raised / jnp.sum(raised, axis=-1, keepdims=True)
    context = einsum("mhqk,mkhd->mqhd", attend.astype(jnp.bfloat16), values)
    context = context.reshape(count, D).astype(jnp.bfloat16)
    return (product(context, wout), (scale, normed, queries, keys, values, context, attend))


def attention_back(grad, rows, gain, wqkv, wout, table, kept):
    scale, normed, queries, keys, values, context, attend = kept
    count = rows.shape[0]
    grad_low = grad.astype(jnp.bfloat16)
    grad_context = (
        product_right(grad_low, wout).astype(jnp.bfloat16).reshape(-1, ROWS, HEADS, HEAD_DIM)
    )
    grad_values = einsum("mhqk,mqhd->mkhd", attend.astype(jnp.bfloat16), grad_context)
    grad_attend = einsum("mqhd,mkhd->mhqk", grad_context, values)
    grad_scores = attend * (grad_attend - jnp.sum(attend * grad_attend, axis=-1, keepdims=True))
    scores_low = grad_scores.astype(jnp.bfloat16)
    grad_bias = jnp.sum(einsum("mhqk,qkb->mhb", scores_low, table), axis=0)
    grad_queries = einsum("mhqk,mkhd->mqhd", scores_low, keys) * FACTOR
    grad_keys = einsum("mhqk,mqhd->mkhd", scores_low, queries) * FACTOR
    grad_mixed = jnp.concatenate(
        [
            item.reshape(count, D).astype(jnp.bfloat16)
            for item in (grad_queries, grad_keys, grad_values)
        ],
        axis=1,
    )
    grad_normed = product_right(grad_mixed, wqkv)
    grad_rows, grad_gain = norm_back(grad_normed, rows, scale, gain)
    return (
        grad_rows,
        (grad_gain, grad_bias.reshape(-1), (normed, grad_mixed), (context, grad_low)),
    )


def feed_forward(rows, gain, w_gate, w_up, w_down):
    normed_full, scale = normalize(rows, gain)
    normed = normed_full.astype(jnp.bfloat16)
    gate = product(normed, w_gate)
    up_part = product(normed, w_up)
    hidden = (jax.nn.gelu(gate, approximate=False) * up_part).astype(jnp.bfloat16)
    return (product(hidden, w_down), (scale, normed, gate, up_part, hidden))


def feed_back(grad, rows, gain, w_gate, w_up, w_down, kept):
    scale, normed, gate, up_part, hidden = kept
    grad_low = grad.astype(jnp.bfloat16)
    grad_hidden = product_right(grad_low, w_down)
    grad_gate = (grad_hidden * up_part * gelu_slope(gate)).astype(jnp.bfloat16)
    grad_up = (grad_hidden * jax.nn.gelu(gate, approximate=False)).astype(jnp.bfloat16)
    grad_normed = product_right(grad_gate, w_gate) + product_right(grad_up, w_up)
    grad_rows, grad_gain = norm_back(grad_normed, rows, scale, gain)
    return (grad_rows, (grad_gain, (normed, grad_gate), (normed, grad_up), (hidden, grad_low)))


def route_table(ids, experts, capacity):
    flat = ids.reshape(MICRO, -1)
    hits = (flat[:, :, None] == jnp.arange(experts, dtype=jnp.int32)).astype(jnp.float32)
    count = flat.shape[1]
    earlier = jnp.tril(jnp.ones((count, count), jnp.bfloat16), -1)
    before = einsum("rs,mse->mre", earlier, hits.astype(jnp.bfloat16))
    slot = jnp.sum(before * hits, axis=2).astype(jnp.int32)
    batch = jnp.arange(MICRO, dtype=jnp.int32)[:, None]
    target = ((flat * MICRO + batch) * capacity + slot).reshape(-1)
    return (
        target[:, None] == jnp.arange(capacity * experts * MICRO, dtype=jnp.int32)[None, :]
    ).astype(jnp.bfloat16)


def body(
    tokens,
    cotangent,
    doc_ids,
    expert_ids,
    gate_logits,
    gain_attn_a,
    gain_mlp,
    gain_attn_b,
    gain_moe,
    bias_a,
    bias_b,
    qkv_a,
    out_a,
    w_gate,
    w_up,
    w_down,
    qkv_b,
    out_b,
    expert_in,
    expert_out,
):
    columns = lax.axis_size("expert")
    layers = lax.axis_size("dp")
    experts = columns * EXP_DEV
    capacity = (2 * ROWS + experts - 1) // experts + 1
    owners = layers * columns
    cube = Cube(layers, columns)
    small = (gain_attn_a, gain_mlp, gain_attn_b, gain_moe, bias_a, bias_b)
    sizes = [item.shape[0] for item in small]
    matrices = (qkv_a, w_gate, w_up, w_down, out_a, qkv_b, out_b)
    whole_tiles = qkv_a.shape[0] % 8 == 0

    packed = jnp.concatenate(small)
    packed = jnp.pad(packed, (0, 128 - packed.shape[0]))
    if whole_tiles:
        tile = jnp.broadcast_to(packed[None], (16, 128))
        full = gather_all(cube, matrices + (tile,))
        smalls = full[7].reshape(owners, 16, 128)[:, 0]
    else:
        full = [lax.all_gather(item, AXES, axis=0, tiled=True) for item in matrices]
        smalls = lax.all_gather(packed, AXES, axis=0)
    qkv_a, w_gate, w_up, w_down, out_a, qkv_b, out_b = full[:7]
    parts, start = [], 0
    for size in sizes:
        parts.append(smalls[:, start : start + size].reshape(-1))
        start += size
    gains = [item.astype(jnp.float32) for item in parts[:4]]
    bias_one, bias_two = (item.reshape(HEADS, BUCKETS) for item in parts[4:])

    rows = tokens.astype(jnp.float32)
    grad = cotangent.astype(jnp.float32)
    mix = jax.nn.softmax(gate_logits, axis=-1)
    allowed, table = layout(doc_ids)
    route = route_table(expert_ids, experts, capacity)
    per_device = EXP_DEV * MICRO * capacity

    def dispatch(values):
        sent = product_left(route, values).astype(jnp.bfloat16)
        sent = sent.reshape(columns, per_device, D)
        arrived = lax.all_to_all(sent, "expert", split_axis=0, concat_axis=0, tiled=True)
        whole = lax.all_gather(arrived, "dp", axis=0, tiled=True)
        whole = whole.reshape(owners, EXP_DEV, MICRO * capacity, D)
        return whole.transpose(1, 0, 2, 3).reshape(EXP_DEV, -1, D)

    def collect(term):
        term = term.astype(jnp.bfloat16).reshape(EXP_DEV, owners, MICRO * capacity, D)
        term = term.transpose(1, 0, 2, 3).reshape(owners, per_device, D)
        summed = lax.psum_scatter(term, "dp", scatter_dimension=0, tiled=True)
        back = lax.all_to_all(summed, "expert", split_axis=0, concat_axis=0, tiled=True)
        return product(route, back.reshape(columns * per_device, D)).reshape(-1, 2, D)

    grad_route = (grad[:, None, :] * mix[:, :, None]).reshape(-1, D).astype(jnp.bfloat16)
    grad_all = dispatch(grad_route)

    attn_one, kept_one = attention_forward(
        rows, gains[0], bias_one, qkv_a, out_a, allowed, table
    )
    first = rows + attn_one
    ffn, kept_ffn = feed_forward(first, gains[1], w_gate, w_up, w_down)
    middle = first + ffn
    attn_two, kept_two = attention_forward(
        middle, gains[2], bias_two, qkv_b, out_b, allowed, table
    )
    second = middle + attn_two
    normed_full, scale_moe = normalize(second, gains[3])
    normed = normed_full.astype(jnp.bfloat16)
    slot_all = dispatch(jnp.repeat(normed, 2, axis=0))
    pre = einsum("erd,edf->erf", slot_all, expert_in)
    act = jax.nn.gelu(pre, approximate=False).astype(jnp.bfloat16)
    per_route = collect(einsum("erf,efd->erd", act, expert_out))
    moe = jnp.sum(per_route * mix[:, :, None], axis=1)
    result = (second + moe).astype(jnp.bfloat16)

    grad_second = einsum("erf,erd->efd", act, grad_all)
    grad_act = einsum("erd,efd->erf", grad_all, expert_out)
    grad_pre = (grad_act * gelu_slope(pre)).astype(jnp.bfloat16)
    grad_first = einsum("erd,erf->edf", slot_all, grad_pre)
    grad_normed = jnp.sum(collect(einsum("erf,edf->erd", grad_pre, expert_in)), axis=1)
    grad_norm_rows, grad_gain_moe = norm_back(grad_normed, second, scale_moe, gains[3])
    grad_second_rows = grad + grad_norm_rows
    back_two, grads_two = attention_back(
        grad_second_rows, middle, gains[2], qkv_b, out_b, table, kept_two
    )
    grad_middle = grad_second_rows + back_two
    back_ffn, grads_ffn = feed_back(
        grad_middle, first, gains[1], w_gate, w_up, w_down, kept_ffn
    )
    grad_first_rows = grad_middle + back_ffn
    back_one, grads_one = attention_back(
        grad_first_rows, rows, gains[0], qkv_a, out_a, table, kept_one
    )
    grad_tokens = grad_first_rows + back_one

    small_grads = (
        grads_one[0],
        grads_ffn[0],
        grads_two[0],
        grad_gain_moe,
        grads_one[1],
        grads_two[1],
    )
    pairs = (
        grads_one[2],
        grads_ffn[1],
        grads_ffn[2],
        grads_ffn[3],
        grads_one[3],
        grads_two[2],
        grads_two[3],
    )
    terms = [product_left(left, right).astype(jnp.bfloat16) for left, right in pairs]
    terms = [item.reshape(owners, -1, item.shape[-1]) for item in terms]
    shared = jnp.concatenate([item.reshape(owners, -1) for item in small_grads], axis=1)
    shared = jnp.pad(shared, ((0, 0), (0, 128 - shared.shape[1])))
    if whole_tiles:
        tile = jnp.broadcast_to(shared[:, None], (owners, 8, 128))
        sums = reduce_all(cube, terms + [tile])
        own_small = sums[7][0]
    else:
        sums = [
            lax.psum_scatter(item, AXES, scatter_dimension=0, tiled=False).astype(jnp.float32)
            for item in terms
        ]
        own_small = lax.psum_scatter(shared, AXES, scatter_dimension=0, tiled=False)
    outs, start = [], 0
    for size in sizes:
        outs.append(own_small[start : start + size])
        start += size
    g_qkv_a, g_gate, g_up, g_down, g_out_a, g_qkv_b, g_out_b = sums[:7]
    return (
        (result, grad_tokens)
        + tuple(outs)
        + (g_qkv_a, g_out_a, g_gate, g_up, g_down, g_qkv_b, g_out_b)
        + (grad_first, grad_second)
    )


def solution(mesh):
    placed = (
        P(("dp", "expert"), None),
        P(("dp", "expert"), None),
        P(("dp", "expert"), None),
        P(("dp", "expert"), None),
        P(("dp", "expert"), None),
        P(("dp", "expert")),
        P(("dp", "expert")),
        P(("dp", "expert")),
        P(("dp", "expert")),
        P(("dp", "expert")),
        P(("dp", "expert")),
        P(("dp", "expert"), None),
        P(("dp", "expert"), None),
        P(("dp", "expert"), None),
        P(("dp", "expert"), None),
        P(("dp", "expert"), None),
        P(("dp", "expert"), None),
        P(("dp", "expert"), None),
        P("expert", None, "dp"),
        P("expert", "dp", None),
    )
    return jax.shard_map(
        body,
        mesh=mesh,
        in_specs=placed,
        out_specs=(
            P(("dp", "expert"), None),
            P(("dp", "expert"), None),
            P(("dp", "expert")),
            P(("dp", "expert")),
            P(("dp", "expert")),
            P(("dp", "expert")),
            P(("dp", "expert")),
            P(("dp", "expert")),
            P(("dp", "expert"), None),
            P(("dp", "expert"), None),
            P(("dp", "expert"), None),
            P(("dp", "expert"), None),
            P(("dp", "expert"), None),
            P(("dp", "expert"), None),
            P(("dp", "expert"), None),
            P("expert", None, "dp"),
            P("expert", "dp", None),
        ),
        check_vma=False,
    )
```

time: 1440 us -> 674 us (0.47)
  waiting for transfers between devices: 853 us -> 41 us
  Pallas kernels: 0 us -> 296 us
  matrix products: 205 us -> 116 us
  blocking collectives: 103 us -> 34.5 us
  starting transfers between devices: 79.2 us -> 11.4 us
  other arithmetic: 58.1 us -> 27.8 us
    all_to_all x20 -> x2, waiting for transfers between devices: 527 us -> 0.01 us  [collect(): lax.all_to_all(summed, 'expert', split_axis=0, concat_axis=0, tiled=True)]
    all_gather x7 -> x2, waiting for transfers between devices: 313 us -> 0.04 us  [dispatch(): whole = lax.all_gather(arrived, 'dp', axis=0, tiled=True)]
    pallas_call x0 -> x2, Pallas kernels: none -> 296 us  [the longest x1 154 us: gather_all(): pl.pallas_call(functools.partial(gather_kernel, cube, count), out_shape=[...]
    all_to_all x20 -> x2, starting transfers between devices: 78.8 us -> 11.3 us  [collect(): lax.all_to_all(summed, 'expert', split_axis=0, concat_axis=0, tiled=True)]
    all_gather x4 -> x0, blocking collectives: 43.1 us -> none  [the longest x2 24.7 us: body(): grad_all = lax.all_gather(grad_arrived, 'dp', axis=0, tiled=True)]
    unnamed x1 -> x0, blocking collectives: 41.5 us -> none
    dot_general x44 -> x23, matrix products: 88 us -> 51.4 us  [einsum(): return jnp.einsum(spec, left, right, preferred_element_type=jnp.float32)]
    unnamed x13 -> x6, waiting for transfers between devices: 4.44 us -> 40.9 us
  transfers between devices with their start and end apart: 31 -> 6, of which waited for: 23 -> 2; matrix products, arithmetic and copies ran while one was open for 16% -> 11% of each run, Pallas kernels for 0% -> 0%
where the time goes in v1:
time: 674 us; the launch traced here: 669 us
  Pallas kernels  296 us (44%)
  local copies, waits for them, and re-layouts  126 us (19%)
  matrix products  116 us (17%)
  waiting for transfers between devices  41 us (6%)
  blocking collectives  34.5 us (5%)
  other arithmetic  27.8 us (4%)
  between operations  15.5 us (2%)
  starting transfers between devices  11.4 us (2%)
    pallas_call x1, Pallas kernels, gather_all(): pl.pallas_call(functools.partial(gather_kernel, cube, count), out_shape=[...  154 us
    pallas_call x1, Pallas kernels, reduce_all(): pl.pallas_call(functools.partial(reduce_kernel, cube, count), out_shape=[...  142 us
    dot_general x23, matrix products, einsum(): return jnp.einsum(spec, left, right, preferred_element_type=jnp.float32)  51.4 us
    unnamed x6, waiting for transfers between devices  40.9 us
    all_to_all x2, blocking collectives, dispatch(): lax.all_to_all(sent, 'expert', split_axis=0, concat_axis=0, tiled=True)  34.5 us
    unnamed x209, local copies, waits for them, and re-layouts  27.8 us
    dot_general x9, matrix products, product(): return jnp.dot(left, right, preferred_element_type=jnp.float32)  25.2 us
    dot_general x9, matrix products, product_left(): lax.dot_general(left, right, (((0,), (0,)), ((), ())), preferred_element_...  23.7 us
  transfers between devices with their start and end apart: 6, of which 2 were waited for; matrix products, arithmetic and copies ran while one was open for 11% of the time, Pallas kernels for 0%

profile of v1, /device:TPU:0, one launch (start us, length us, event | category | flops | bytes accessed | tf_op | source)
XLA Modules:
  0.0 668.7 jit_solution(1595795067854955043)
XLA Ops:
  7.2 4.1 concatenate.12
  11.9 154.4 %shard_map.323 = (bf16[2,2,2,2,2,24,2304]{6,5,4,3,2,1,0:T(8,128)(2,1)}, bf16[2,2,2,2,2,24,3072]{6,5,4,3,2,1,0:T(8,128)(2,1)}, bf16[2,2,2,2,2,24,3072]{6,5,4,3,2,...) custom-call(bf16[24,2304]{1,0:T(8,128)(2,1)} %refs_0_.1, ...), custom_call_target="tpu_custom_call" | custom-call | tf_op jit(solution)/shard_map/pallas_call | solution.py:114
  170.3 2.8 convolution_convert_fusion.6
  183.6 3.3 fusion.135
  188.1 8.2 %multiply_convert_fusion.1 = (bf16[128,3072]{1,0:T(8,128)(2,1)S(1)}, f32[128,3072]{1,0:T(8,128)}, f32[128,3072]{1,0:T(8,128)}) fusion(f32[128,3072]{1,0:T(8,128)S(1)} %fusion.135, bf16[128,768]{1,0:T(8,128)(2,1)S(1)} %multiply_convert_fusion.8, bf16[768,3072]{1,0:T(8,128)(2,1)} %bitcast.261), kind=kOutput, calls=%fused_computation.58 | convolution fusion | flops 629932032 | bytes 10420224 | tf_op jit(solution)/shard_map/dot_general | solution.py:241
  199.9 2.5 convolution_convert_fusion.5
  202.4 2.1 copy.147
  204.5 3.4 reshape.345
  207.9 3.3 fusion.129
  211.2 1.9 copy.232
  213.1 2.1 copy.233
  216.6 2.0 fusion.136
  218.6 2.0 copy.152
  224.1 2.6 fusion.53
  226.7 2.1 copy.154
  228.8 1.9 convert_element_type.269
  230.7 2.5 multiply_reduce_fusion.8
  237.2 1.9 reshape.347
  252.9 17.0 %all_to_all.20 = bf16[8,40,768]{2,1,0:T(8,128)(2,1)S(1)} all-to-all(bf16[8,40,768]{2,1,0:T(8,128)(2,1)S(1)} %bitcast.268), channel_id=1, replica_groups=mesh['dp'=4,'expert'=8] {'expert'}, dimensions={0} | all-to-all | bytes 983040 | tf_op jit(solution)/shard_map/all_to_all | solution.py:434
  277.0 2.0 mul.411
  279.0 2.6 mul.412
  283.1 17.5 %all_to_all.21 = bf16[8,40,768]{2,1,0:T(8,128)(2,1)S(1)} all-to-all(bf16[8,40,768]{2,1,0:T(8,128)(2,1)S(1)} %bitcast.267), channel_id=1, replica_groups=mesh['dp'=4,'expert'=8] {'expert'}, dimensions={0} | all-to-all | bytes 983040 | tf_op jit(solution)/shard_map/all_to_all | solution.py:434
  301.6 3.1 copy.159
  304.7 6.0 fusion.67
  310.7 9.4 %fusion.4 = bf16[4,320,768]{2,1,0:T(8,128)(2,1)S(1)} fusion(f32[4,320,768]{2,1,0:T(8,128)S(1)} %get-tuple-element.96, u8[320,768]{1,0:T(8,128)(4,1)S(1)} %get-tuple-element.50, u8[320,768]{1,0:T(8,128)(4,1)S(1)} %get-tuple-element.49), kind=kLoop, calls=%fused_computation.11 | loop fusion | flops 68812800 | bytes 6389760 | tf_op jit(solution)/shard_map/convert_element_type | solution.py:463
  325.4 3.2 copy.166
  329.9 4.5 fusion.10
  334.4 1.7 convolution_convert_fusion.7
  339.6 15.9 %reduce-scatter.7.cloned.1.call-done = bf16[8,30720]{1,0:T(8,128)(2,1)} async-done(((bf16[32,30720]{1,0:T(8,128)(2,1)}), bf16[8,30720]{1,0:T(8,128)(2,1)}) %reduce-scatter.7.cloned.1.call-update) | async-done | bytes 491536
  355.5 1.9 copy.163
  357.4 5.5 all-to-all-start.1
  364.4 25.0 %reduce-scatter.9.cloned.1.call-done = bf16[8,30720]{1,0:T(8,128)(2,1)} async-done(((bf16[32,30720]{1,0:T(8,128)(2,1)}), bf16[8,30720]{1,0:T(8,128)(2,1)}) %reduce-scatter.9.cloned.1.call-update) | async-done | bytes 491536
  389.3 1.9 copy.170
  391.2 5.8 all-to-all-start.3
  397.0 8.7 %fusion.20 = f32[4,768,768]{2,1,0:T(8,128)} fusion(bf16[4,320,768]{2,1,0:T(8,128)(2,1)} %copy-done.29, bf16[4,320,768]{2,0,1:T(4,128)(2,1)} %bitcast.246), kind=kOutput, calls=%fused_computation.45 | convolution fusion | flops 1509949440 | bytes 13369344 | tf_op jit(solution)/shard_map/erd,erf->edf/dot_general | solution.py:257
  405.7 5.2 fusion.17
  410.9 2.2 fusion.47
  414.8 1.8 multiply_reduce_fusion.2
  416.6 2.0 multiply_add_fusion.2
  420.6 2.1 reshape.384
  422.6 2.1 copy.182
  424.8 2.6 fusion.54
  427.4 1.8 multiply_reduce_fusion.1
  432.7 1.9 convert_element_type.298
  434.6 1.9 copy.181
  436.5 1.9 convert_element_type.295
  438.5 2.1 copy.177
  440.6 1.9 convert_element_type.292
  445.6 3.0 multiply_reduce_fusion.3
  448.9 4.3 multiply_convert_fusion
  455.0 1.8 multiply_reduce_fusion.4
  459.0 2.7 fusion.55
  469.2 3.0 convolution_convert_fusion
  473.7 3.6 convolution_convert_fusion.1
  477.4 3.9 convolution_convert_fusion.2
  481.2 3.6 convolution_convert_fusion.3
  486.0 1.9 convert_element_type.313
  488.0 1.9 copy.195
  489.9 1.9 convert_element_type.310
  491.8 1.9 copy.191
  493.7 1.9 convert_element_type.307
  498.5 3.6 fusion.81
  502.1 3.6 convolution_convert_fusion.4
  507.0 141.6 %shard_map.324 = (f32[24,2304]{1,0:T(8,128)}, f32[24,3072]{1,0:T(8,128)}, f32[24,3072]{1,0:T(8,128)}, f32[96,768]{1,0:T(8,128)}, f32[24,768]{1,0:T(8,128)}, /*in...) custom-call(bf16[2,2,2,2,2,24,2304]{6,5,4,3,2,1,0:T(8,128)(2,1)} %bitcast.244, ...), custom_call_target="tpu_custom_call" | custom-call | tf_op jit(solution)/shard_map/pallas_call | solution.py:223
  (326 shorter events, 104.7 us)
Async XLA Ops:
  7.2 294.4 %all-gather.3.cloned.1.call-start = ((), (), s32[]{:S(2)}) async-start(), calls=%async_computation.6 | async-start | bytes 2457600 | tf_op jit(solution)/shard_map/all_gather | solution.py:435
  168.6 7.9 %copy-start.59 = (s32[64,64]{0,1:T(8,128)}, s32[64,64]{0,1:T(8,128)S(1)}, u32[]{:S(2)}) copy-start(s32[64,64]{0,1:T(8,128)S(1)} %fusion.118) | copy-start | bytes 49156
  169.2 4.7 copy-start.61
  173.9 4.5 copy-start.82
  175.4 4.7 copy-start.53
  176.0 5.2 copy-start.32
  179.0 4.3 copy-start.43
  179.0 3.9 copy-start.12
  179.0 3.9 copy-start.26
  182.8 4.0 copy-start.47
  183.6 12.8 %slice-start.2 = ((s8[4718592]{0:T(1024)(128)(4,1)}), s8[4194304]{0:T(1024)(128)(4,1)S(1)}, s32[]{:S(2)}) async-start(s8[4718592]{0:T(1024)(128)(4,1)} %bitcast.236), calls=%async_computation.12 | async-start | bytes 8388608
  188.1 8.3 %slice-start.3 = ((s8[4718592]{0:T(1024)(128)(4,1)}), s8[524288]{0:T(1024)(128)(4,1)S(1)}, s32[]{:S(2)}) async-start(s8[4718592]{0:T(1024)(128)(4,1)} %bitcast.236), calls=%async_computation.13 | async-start | bytes 1048576
  188.1 8.3 %copy-start.10 = (f32[128,768]{1,0:T(8,128)S(1)}, f32[128,768]{1,0:T(8,128)}, u32[]{:S(2)}) copy-start(f32[128,768]{1,0:T(8,128)} %copy-done.9) | copy-start | bytes 1179652
  270.8 54.5 %all-gather.5.cloned.1.call-start = ((), (), s32[]{:S(2)}) async-start(), calls=%async_computation.7 | async-start | bytes 2457600 | tf_op jit(solution)/shard_map/all_gather | solution.py:435
  301.5 54.0 %reduce-scatter.7.cloned.1.call-start = ((), (), s32[]{:S(2)}) async-start(), calls=%async_computation.8 | async-start | bytes 2457600
  304.7 6.0 copy-start.4
  304.7 15.5 %slice-start.6 = ((s8[4718592]{0:T(1024)(128)(4,1)}), s8[4194304]{0:T(1024)(128)(4,1)S(1)}, s32[]{:S(2)}) async-start(s8[4718592]{0:T(1024)(128)(4,1)} %bitcast.275), calls=%async_computation.16 | async-start | bytes 8388608
  304.7 15.5 %slice-start.7 = ((s8[4718592]{0:T(1024)(128)(4,1)}), s8[524288]{0:T(1024)(128)(4,1)S(1)}, s32[]{:S(2)}) async-start(s8[4718592]{0:T(1024)(128)(4,1)} %bitcast.275), calls=%async_computation.17 | async-start | bytes 1048576
  310.7 11.2 %copy-start.30 = (f32[4,320,768]{2,1,0:T(8,128)}, f32[4,320,768]{2,1,0:T(8,128)S(1)}, u32[]{:S(2)}) copy-start(f32[4,320,768]{2,1,0:T(8,128)S(1)} %get-tuple-element.96) | copy-start | bytes 11796484
  325.3 64.0 %reduce-scatter.9.cloned.1.call-start = ((), (), s32[]{:S(2)}) async-start(), calls=%async_computation.9 | async-start | bytes 2457600
  325.4 4.6 copy-start.31
  325.4 9.0 %slice-start.8 = ((s8[4718592]{0:T(1024)(128)(4,1)}), s8[4194304]{0:T(1024)(128)(4,1)S(1)}, s32[]{:S(2)}) async-start(s8[4718592]{0:T(1024)(128)(4,1)} %bitcast.277), calls=%async_computation.18 | async-start | bytes 8388608
  329.9 4.5 slice-start.9
  357.4 33.9 %all-to-all-start.1 = ((bf16[8,40,768]{2,1,0:T(8,128)(2,1)}), bf16[8,40,768]{2,1,0:T(8,128)(2,1)}, u32[]{:S(2)}, u32[]{:S(2)}) async-start(bf16[8,40,768]{2,1,0:T(8,128)(2,1)} %copy.163), calls=%async_computation.1 | async-start | bytes 983040 | tf_op jit(solution)/shard_map/all_to_all | solution.py:443
  391.2 21.9 %all-to-all-start.3 = ((bf16[8,40,768]{2,1,0:T(8,128)(2,1)}), bf16[8,40,768]{2,1,0:T(8,128)(2,1)}, u32[]{:S(2)}, u32[]{:S(2)}) async-start(bf16[8,40,768]{2,1,0:T(8,128)(2,1)} %copy.170), calls=%async_computation.3 | async-start | bytes 983040 | tf_op jit(solution)/shard_map/all_to_all | solution.py:443
  397.0 8.7 %copy-start.6 = (bf16[4,320,768]{2,1,0:T(8,128)(2,1)S(1)}, bf16[4,320,768]{2,1,0:T(8,128)(2,1)}, u32[]{:S(2)}) copy-start(bf16[4,320,768]{2,1,0:T(8,128)(2,1)} %copy-done.5) | copy-start | bytes 5898244
  397.0 8.7 %copy-start.8 = (bf16[4,32,10,768]{3,0,2,1:T(4,128)(2,1)S(1)}, bf16[4,32,10,768]{3,0,2,1:T(4,128)(2,1)}, u32[]{:S(2)}) copy-start(bf16[4,32,10,768]{3,0,2,1:T(4,128)(2,1)} %copy-done.7) | copy-start | bytes 5898244
  405.7 5.2 copy-start.80
  405.7 5.2 copy-start.83
  413.2 6.2 copy-start.28
  427.4 4.1 copy-start.57
  430.5 15.1 %copy-start.63 = (f32[768]{0:T(1024)S(1)}, f32[768]{0:T(1024)}, u32[]{:S(2)}) copy-start(f32[768]{0:T(1024)} %reshape.368) | copy-start | bytes 9220
  430.5 15.1 %copy-start.77 = (f32[128]{0:T(128)S(1)}, f32[128]{0:T(128)}, u32[]{:S(2)}) copy-start(f32[128]{0:T(128)} %add_rsqrt_fusion.1) | copy-start | bytes 1540
  442.5 6.2 copy-start.2
  442.5 6.2 copy-start.18
  444.5 4.4 copy-start.21
  444.5 4.4 copy-start.50
  444.5 4.4 copy-start.51
  445.6 7.6 %slice-start = ((s8[4718592]{0:T(1024)(128)(4,1)}), s8[4194304]{0:T(1024)(128)(4,1)S(1)}, s32[]{:S(2)}) async-start(s8[4718592]{0:T(1024)(128)(4,1)} %bitcast.232), calls=%async_computation.10 | async-start | bytes 8388608
  445.6 9.3 %slice-start.4 = ((s8[4718592]{0:T(1024)(128)(4,1)}), s8[4194304]{0:T(1024)(128)(4,1)S(1)}, s32[]{:S(2)}) async-start(s8[4718592]{0:T(1024)(128)(4,1)} %bitcast.262), calls=%async_computation.14 | async-start | bytes 8388608
  448.9 4.3 slice-start.1
  448.9 6.0 slice-start.5
  457.0 15.2 %copy-start.15 = (f32[128,768]{1,0:T(8,128)}, f32[128,768]{1,0:T(8,128)S(1)}, u32[]{:S(2)}) copy-start(f32[128,768]{1,0:T(8,128)S(1)} %multiply_add_fusion) | copy-start | bytes 1179652
  457.0 4.7 copy-start.54
  461.7 3.9 copy-start.60
  463.3 4.4 copy-start.19
  463.3 4.4 copy-start.49
  463.5 5.7 copy-start.3
  463.5 5.7 copy-start.41
  466.6 5.6 copy-start.48
  469.2 4.5 copy-start.25
  484.8 13.7 %copy-start = (bf16[2,2,2,2,2,24,2304]{6,5,4,3,2,1,0:T(8,128)(2,1)S(1)}, bf16[2,2,2,2,2,24,2304]{6,5,4,3,2,1,0:T(8,128)(2,1)}, u32[]{:S(2)}) copy-start(bf16[2,2,2,2,2,24,2304]{6,5,4,3,2,1,0:T(8,128)(2,1)} %get-tuple-element.34) | copy-start | bytes 10616836
  484.8 13.7 %copy-start.62 = (f32[768]{0:T(1024)S(1)}, f32[768]{0:T(1024)}, u32[]{:S(2)}) copy-start(f32[768]{0:T(1024)} %copy-done.61) | copy-start | bytes 9220
  495.6 6.5 copy-start.13
  498.5 7.6 %copy-start.70 = (f32[768]{0:T(1024)S(1)}, f32[768]{0:T(1024)}, u32[]{:S(2)}) copy-start(f32[768]{0:T(1024)} %get-tuple-element.51) | copy-start | bytes 9220
  502.1 3.7 copy-start.74
  502.1 3.9 copy-start.73
  507.0 144.4 %copy-start.84 = (f32[128]{0:T(128)S(1)}, f32[128]{0:T(128)}, u32[]{:S(2)}) copy-start(f32[128]{0:T(128)} %get-tuple-element.58) | copy-start | bytes 1540
  507.0 144.4 %copy-start.14 = (bf16[128,768]{1,0:T(8,128)(2,1)S(1)}, bf16[128,768]{1,0:T(8,128)(2,1)}, u32[]{:S(2)}) copy-start(bf16[128,768]{1,0:T(8,128)(2,1)} %param.20) | copy-start | bytes 589828
  507.0 144.4 %copy-start.16 = (f32[128,768]{1,0:T(8,128)S(1)}, f32[128,768]{1,0:T(8,128)}, u32[]{:S(2)}) copy-start(f32[128,768]{1,0:T(8,128)} %copy-done.15) | copy-start | bytes 1179652
  507.0 144.4 %copy-start.52 = (f32[128,768]{1,0:T(8,128)S(1)}, f32[128,768]{1,0:T(8,128)}, u32[]{:S(2)}) copy-start(f32[128,768]{1,0:T(8,128)} %get-tuple-element.103) | copy-start | bytes 1179652
  507.0 144.4 %copy-start.76 = (f32[128]{0:T(128)S(1)}, f32[128]{0:T(128)}, u32[]{:S(2)}) copy-start(f32[128]{0:T(128)} %copy-done.75) | copy-start | bytes 1540
  648.6 12.0 %copy-start.58 = (f32[24,2304]{1,0:T(8,128)S(1)}, f32[24,2304]{1,0:T(8,128)}, u32[]{:S(2)}) copy-start(f32[24,2304]{1,0:T(8,128)} %get-tuple-element.134) | copy-start | bytes 663556
  648.6 12.7 %copy-start.64 = (f32[24,768]{1,0:T(8,128)S(1)}, f32[24,768]{1,0:T(8,128)}, u32[]{:S(2)}) copy-start(f32[24,768]{1,0:T(8,128)} %get-tuple-element.135) | copy-start | bytes 221188
  (37 other events, 85.0 us)
Sparse Core Ops, SparseCore 0:
  270.9 19.9 all-gather.2
  301.7 19.9 all-gather.4
  325.4 30.0 reduce-scatter.6
  358.7 30.6 reduce-scatter.8

commit v2 on v1

--- a/solution.py
+++ b/solution.py
@@ -401,7 +401,7 @@
     cube = Cube(layers, columns)
     small = (gain_attn_a, gain_mlp, gain_attn_b, gain_moe, bias_a, bias_b)
     sizes = [item.shape[0] for item in small]
-    matrices = (qkv_a, w_gate, w_up, w_down, out_a, qkv_b, out_b)
+    matrices = (qkv_a, w_gate, w_up, w_down, out_a)
     whole_tiles = qkv_a.shape[0] % 8 == 0
 
     packed = jnp.concatenate(small)
@@ -409,11 +409,13 @@
     if whole_tiles:
         tile = jnp.broadcast_to(packed[None], (16, 128))
         full = gather_all(cube, matrices + (tile,))
-        smalls = full[7].reshape(owners, 16, 128)[:, 0]
+        smalls = full[5].reshape(owners, 16, 128)[:, 0]
     else:
         full = [lax.all_gather(item, AXES, axis=0, tiled=True) for item in matrices]
         smalls = lax.all_gather(packed, AXES, axis=0)
-    qkv_a, w_gate, w_up, w_down, out_a, qkv_b, out_b = full[:7]
+    qkv_a, w_gate, w_up, w_down, out_a = full[:5]
+    qkv_b = lax.all_gather(qkv_b, AXES, axis=0, tiled=True)
+    out_b = lax.all_gather(out_b, AXES, axis=0, tiled=True)
     parts, start = [], 0
     for size in sizes:
         parts.append(smalls[:, start : start + size].reshape(-1))
@@ -436,10 +438,12 @@
         whole = whole.reshape(owners, EXP_DEV, MICRO * capacity, D)
         return whole.transpose(1, 0, 2, 3).reshape(EXP_DEV, -1, D)
 
-    def collect(term):
+    def collect_sum(term):
         term = term.astype(jnp.bfloat16).reshape(EXP_DEV, owners, MICRO * capacity, D)
         term = term.transpose(1, 0, 2, 3).reshape(owners, per_device, D)
-        summed = lax.psum_scatter(term, "dp", scatter_dimension=0, tiled=True)
+        return lax.psum_scatter(term, "dp", scatter_dimension=0, tiled=True)
+
+    def collect_back(summed):
         back = lax.all_to_all(summed, "expert", split_axis=0, concat_axis=0, tiled=True)
         return product(route, back.reshape(columns * per_device, D)).reshape(-1, 2, D)
 
@@ -461,21 +465,31 @@
     slot_all = dispatch(jnp.repeat(normed, 2, axis=0))
     pre = einsum("erd,edf->erf", slot_all, expert_in)
     act = jax.nn.gelu(pre, approximate=False).astype(jnp.bfloat16)
-    per_route = collect(einsum("erf,efd->erd", act, expert_out))
-    moe = jnp.sum(per_route * mix[:, :, None], axis=1)
-    result = (second + moe).astype(jnp.bfloat16)
+    term = einsum("erf,efd->erd", act, expert_out).astype(jnp.bfloat16)
 
     grad_second = einsum("erf,erd->efd", act, grad_all)
     grad_act = einsum("erd,efd->erf", grad_all, expert_out)
     grad_pre = (grad_act * gelu_slope(pre)).astype(jnp.bfloat16)
     grad_first = einsum("erd,erf->edf", slot_all, grad_pre)
-    grad_normed = jnp.sum(collect(einsum("erf,edf->erd", grad_pre, expert_in)), axis=1)
+    summed_grad = collect_sum(einsum("erf,edf->erd", grad_pre, expert_in))
+    term, summed_grad = lax.optimization_barrier((term, summed_grad))
+    summed = collect_sum(term)
+    grad_normed = jnp.sum(collect_back(summed_grad), axis=1)
     grad_norm_rows, grad_gain_moe = norm_back(grad_normed, second, scale_moe, gains[3])
     grad_second_rows = grad + grad_norm_rows
     back_two, grads_two = attention_back(
         grad_second_rows, middle, gains[2], qkv_b, out_b, table, kept_two
     )
     grad_middle = grad_second_rows + back_two
+    grad_middle, summed = lax.optimization_barrier((grad_middle, summed))
+    moe = jnp.sum(collect_back(summed) * mix[:, :, None], axis=1)
+    result = (second + moe).astype(jnp.bfloat16)
+    g_qkv_b, g_out_b = (
+        lax.psum_scatter(
+            product_left(left, right).astype(jnp.bfloat16), AXES, scatter_dimension=0, tiled=True
+        ).astype(jnp.float32)
+        for left, right in grads_two[2:4]
+    )
     back_ffn, grads_ffn = feed_back(
         grad_middle, first, gains[1], w_gate, w_up, w_down, kept_ffn
     )
@@ -499,8 +513,6 @@
         grads_ffn[2],
         grads_ffn[3],
         grads_one[3],
-        grads_two[2],
-        grads_two[3],
     )
     terms = [product_left(left, right).astype(jnp.bfloat16) for left, right in pairs]
     terms = [item.reshape(owners, -1, item.shape[-1]) for item in terms]
@@ -509,7 +521,7 @@
     if whole_tiles:
         tile = jnp.broadcast_to(shared[:, None], (owners, 8, 128))
         sums = reduce_all(cube, terms + [tile])
-        own_small = sums[7][0]
+        own_small = sums[5][0]
     else:
         sums = [
             lax.psum_scatter(item, AXES, scatter_dimension=0, tiled=False).astype(jnp.float32)
@@ -520,7 +532,7 @@
     for size in sizes:
         outs.append(own_small[start : start + size])
         start += size
-    g_qkv_a, g_gate, g_up, g_down, g_out_a, g_qkv_b, g_out_b = sums[:7]
+    g_qkv_a, g_gate, g_up, g_down, g_out_a = sums[:5]
     return (
         (result, grad_tokens)
         + tuple(outs)

time: 674 us -> 681 us (1.010)
  waiting for transfers between devices: 41 us -> 119 us
  local copies, waits for them, and re-layouts: 126 us -> 81.1 us
  Pallas kernels: 296 us -> 273 us
  blocking collectives: 34.5 us -> 17.1 us
  matrix products: 116 us -> 124 us
  starting transfers between devices: 11.4 us -> 19.4 us
    reduce_scatter x0 -> x2, waiting for transfers between devices: none -> 40.2 us  [body(): lax.psum_scatter(product_left(left, right).astype(jnp.bfloat16), AXES, sc...]
    all_gather x2, waiting for transfers between devices: 0.04 us -> 18.5 us  [dispatch(): whole = lax.all_gather(arrived, 'dp', axis=0, tiled=True)]
    pallas_call x1, Pallas kernels: 142 us -> 124 us  [reduce_all(): pl.pallas_call(functools.partial(reduce_kernel, cube, count), out_shape=[...]
    all_to_all x2 -> x1, blocking collectives: 34.5 us -> 17.1 us  [dispatch(): lax.all_to_all(sent, 'expert', split_axis=0, concat_axis=0, tiled=True)]
    all_to_all x2 -> x3, waiting for transfers between devices: 0.01 us -> 13.8 us  [the longest x2 13.8 us: collect_back(): lax.all_to_all(summed, 'expert', split_axis=0, concat_axis=0, tiled=True)]
    unnamed x209 -> x201, local copies, waits for them, and re-layouts: 27.8 us -> 17.4 us
    all_to_all x2 -> x3, starting transfers between devices: 11.3 us -> 18.7 us  [the longest x2 11.4 us: collect_back(): lax.all_to_all(summed, 'expert', split_axis=0, concat_axis=0, tiled=True)]
    unnamed x6 -> x10, waiting for transfers between devices: 40.9 us -> 46.4 us
  transfers between devices with their start and end apart: 6 -> 11, of which waited for: 2 -> 5; matrix products, arithmetic and copies ran while one was open for 11% -> 29% of each run, Pallas kernels for 0% -> 40%
where the time goes in v2:
time: 681 us; the launch traced here: 675 us
  Pallas kernels  273 us (40%)
  matrix products  124 us (18%)
  waiting for transfers between devices  119 us (17%)
  local copies, waits for them, and re-layouts  81.1 us (12%)
  other arithmetic  26.2 us (4%)
  starting transfers between devices  19.4 us (3%)
  blocking collectives  17.1 us (3%)
  between operations  16 us (2%)
    pallas_call x1, Pallas kernels, gather_all(): pl.pallas_call(functools.partial(gather_kernel, cube, count), out_shape=[...  149 us
    pallas_call x1, Pallas kernels, reduce_all(): pl.pallas_call(functools.partial(reduce_kernel, cube, count), out_shape=[...  124 us
    dot_general x23, matrix products, einsum(): return jnp.einsum(spec, left, right, preferred_element_type=jnp.float32)  52.2 us
    unnamed x10, waiting for transfers between devices  46.4 us
    reduce_scatter x2, waiting for transfers between devices, body(): lax.psum_scatter(product_left(left, right).astype(jnp.bfloat16), AXES, sc...  40.2 us
    dot_general x9, matrix products, product_left(): lax.dot_general(left, right, (((0,), (0,)), ((), ())), preferred_element_...  26.2 us
    dot_general x9, matrix products, product(): return jnp.dot(left, right, preferred_element_type=jnp.float32)  25.8 us
    dot_general x7, matrix products, product_right(): lax.dot_general(left, right, (((1,), (1,)), ((), ())), preferred_element_...  19.6 us
  transfers between devices with their start and end apart: 11, of which 5 were waited for; matrix products, arithmetic and copies ran while one was open for 29% of the time, Pallas kernels for 40%

profile of v2, /device:TPU:0, one launch (start us, length us, event | category | flops | bytes accessed | tf_op | source)
XLA Modules:
  0.0 675.3 jit_solution(15133431084460412995)
XLA Ops:
  15.9 7.3 %all-to-all-start.1 = ((bf16[8,40,768]{2,1,0:T(8,128)(2,1)}), bf16[8,40,768]{2,1,0:T(8,128)(2,1)S(1)}, u32[]{:S(2)}, u32[]{:S(2)}) async-start(bf16[8,40,768]{2,1,0:T(8,128)(2,1)} %bitcast.24), calls=%async_computation.1 | async-start | bytes 983040 | tf_op jit(solution)/shard_map/all_to_all | solution.py:436
  24.9 149.0 %shard_map.323 = (bf16[2,2,2,2,2,24,2304]{6,5,4,3,2,1,0:T(8,128)(2,1)}, bf16[2,2,2,2,2,24,3072]{6,5,4,3,2,1,0:T(8,128)(2,1)}, bf16[2,2,2,2,2,24,3072]{6,5,4,3,2,...) custom-call(bf16[24,2304]{1,0:T(8,128)(2,1)} %refs_0_.1, ...), custom_call_target="tpu_custom_call" | custom-call | tf_op jit(solution)/shard_map/pallas_call | solution.py:114
  179.1 2.7 convolution_convert_fusion.6
  182.6 2.0 fusion.130
  188.6 2.1 fusion.52
  190.7 2.2 copy.146
  194.8 3.2 fusion.135
  198.1 8.8 %multiply_convert_fusion.1 = (bf16[128,3072]{1,0:T(8,128)(2,1)S(1)}, f32[128,3072]{1,0:T(8,128)}, f32[128,3072]{1,0:T(8,128)}) fusion(f32[128,3072]{1,0:T(8,128)S(1)} %fusion.135, bf16[128,768]{1,0:T(8,128)(2,1)S(1)} %multiply_convert_fusion.8, bf16[768,3072]{1,0:T(8,128)(2,1)} %bitcast.249), kind=kOutput, calls=%fused_computation.58 | convolution fusion | flops 629932032 | bytes 10420224 | tf_op jit(solution)/shard_map/dot_general | solution.py:241
  207.7 3.2 multiply_reduce_fusion.9
  212.1 2.7 convolution_convert_fusion.5
  215.6 2.0 fusion.129
  218.8 1.9 fusion.133
  222.4 1.8 multiply_reduce_fusion.8
  225.2 17.1 %all_to_all.20 = bf16[8,40,768]{2,1,0:T(8,128)(2,1)S(1)} all-to-all(bf16[8,40,768]{2,1,0:T(8,128)(2,1)S(1)} %bitcast.253), channel_id=1, replica_groups=mesh['dp'=4,'expert'=8] {'expert'}, dimensions={0} | all-to-all | bytes 983040 | tf_op jit(solution)/shard_map/all_to_all | solution.py:436
  243.2 3.1 copy.163
  246.3 18.5 %all-gather.9.cloned.1.call-done = bf16[32,40,768]{2,0,1:T(8,128)(2,1)} async-done(((bf16[8,40,768]{2,0,1:T(8,128)(2,1)}), bf16[32,40,768]{2,0,1:T(8,128)(2,1)}) %all-gather.9.cloned.1.call-update) | async-done | bytes 1966096 | tf_op jit(solution)/shard_map/all_gather | solution.py:437
  264.8 3.2 copy.159
  268.1 6.5 fusion.67
  274.6 3.2 fusion.10
  277.9 1.7 convolution_convert_fusion.7
  279.6 1.5 copy.165
  283.0 10.2 %fusion.4 = bf16[4,320,768]{2,1,0:T(8,128)(2,1)S(1)} fusion(f32[4,320,768]{2,1,0:T(8,128)} %copy-done.32, u8[320,768]{1,0:T(8,128)(4,1)} %get-tuple-element.50, u8[320,768]{1,0:T(8,128)(4,1)S(1)} %get-tuple-element.49), kind=kLoop, calls=%fused_computation.11 | loop fusion | flops 68812800 | bytes 6389760 | tf_op jit(solution)/shard_map/convert_element_type | solution.py:467
  294.5 5.3 convolution_convert_fusion.8
  299.9 13.9 %reduce-scatter.13.cloned.1.call-done = bf16[8,30720]{1,0:T(8,128)(2,1)} async-done(((bf16[32,30720]{1,0:T(8,128)(2,1)}), bf16[8,30720]{1,0:T(8,128)(2,1)}) %reduce-scatter.13.cloned.1.call-update) | async-done | bytes 491536
  313.8 1.9 copy.167
  315.7 5.5 all-to-all-start.2
  321.3 13.8 %all-to-all-done.2 = bf16[8,40,768]{2,1,0:T(8,128)(2,1)} async-done(((bf16[8,40,768]{2,1,0:T(8,128)(2,1)}), bf16[8,40,768]{2,1,0:T(8,128)(2,1)}, u32[]{:S(2)}, u32[]{:S(2)}) %all-to-all-start.2) | async-done | bytes 491552 | tf_op jit(solution)/shard_map/all_to_all | solution.py:447
  335.1 1.5 convolution_reduce_fusion
  338.4 2.6 convolution_convert_fusion.9
  341.1 3.1 copy.182
  346.1 8.1 %fusion.17 = f32[4,768,768]{2,1,0:T(8,128)} fusion(bf16[4,320,768]{2,1,0:T(8,128)(2,1)} %copy-done.5, bf16[4,320,768]{2,0,1:T(4,128)(2,1)S(1)} %bitcast.237), kind=kOutput, calls=%fused_computation.42 | convolution fusion | flops 1509949440 | bytes 13369344 | tf_op jit(solution)/shard_map/erf,erd->efd/dot_general | solution.py:257
  354.3 5.4 fusion.20
  361.7 1.8 fusion.54
  366.1 2.2 fusion.57
  368.2 1.9 copy.178
  370.1 1.9 convert_element_type.298
  372.1 2.2 fusion.59
  374.2 1.9 copy.174
  376.2 1.9 convert_element_type.295
  378.1 2.0 fusion.63
  384.4 3.8 multiply_reduce_fusion.3
  390.9 4.4 convolution_convert_fusion
  395.3 40.2 %reduce-scatter.11.cloned.1.call-done = bf16[24,768]{1,0:T(8,128)(2,1)} async-done(((bf16[768,768]{1,0:T(8,128)(2,1)}), bf16[24,768]{1,0:T(8,128)(2,1)}) %reduce-scatter.11.cloned.1.call-update) | async-done | bytes 36880 | tf_op jit(solution)/shard_map/reduce_scatter | solution.py:488
  436.9 31.1 %reduce-scatter.15.cloned.1.call-done = bf16[8,30720]{1,0:T(8,128)(2,1)} async-done(((bf16[32,30720]{1,0:T(8,128)(2,1)}), bf16[8,30720]{1,0:T(8,128)(2,1)}) %reduce-scatter.15.cloned.1.call-update) | async-done | bytes 491536
  468.0 5.1 multiply_convert_fusion
  473.2 1.7 fusion.137
  475.8 4.2 multiply_reduce_fusion.4
  481.6 5.9 all-to-all-start.3
  488.2 1.8 fusion.55
  493.3 2.2 fusion.58
  495.5 1.9 copy.191
  497.4 1.9 convert_element_type.311
  499.3 2.1 fusion.56
  501.5 1.9 copy.195
  503.4 1.9 convert_element_type.314
  510.3 3.7 fusion.81
  515.1 2.6 convolution_convert_fusion.10
  517.7 4.1 convolution_convert_fusion.4
  521.9 3.6 convolution_convert_fusion.2
  525.4 3.6 convolution_convert_fusion.3
  529.0 3.6 convolution_convert_fusion.1
  533.4 123.7 %shard_map.324 = (f32[24,2304]{1,0:T(8,128)}, f32[24,3072]{1,0:T(8,128)}, f32[24,3072]{1,0:T(8,128)}, f32[96,768]{1,0:T(8,128)}, f32[24,768]{1,0:T(8,128)}, /*index=5*/f32[8,128]{1,0:T(8,128)}) custom-call(bf16[2,2,2,2,2,24,2304]{6,5,4,3,2,1,0:T(8,128)(2,1)} %bitcast.233, bf16[2,2,2,2,2,24,3072]{6,5,4,3,2,1,0:T(8,128)(2,1)} %bitcast.225, ...), custom_call_target="tpu_custom_call" | custom-call | tf_op jit(solution)/shard_map/pallas_call | solution.py:223
  660.9 1.5 fusion.47
  663.1 1.6 convert_element_type.324
  (332 shorter events, 70.3 us)
Async XLA Ops:
  7.2 16.9 %copy-start.84 = (bf16[12]{0:T(256)(128)(2,1)S(1)}, bf16[12]{0:T(256)(128)(2,1)}, u32[]{:S(2)}) copy-start(bf16[12]{0:T(256)(128)(2,1)} %param.30) | copy-start | bytes 76
  7.2 16.9 %copy-start.83 = (bf16[12]{0:T(256)(128)(2,1)S(1)}, bf16[12]{0:T(256)(128)(2,1)}, u32[]{:S(2)}) copy-start(bf16[12]{0:T(256)(128)(2,1)} %param.29) | copy-start | bytes 76
  7.2 16.9 %copy-start.82 = (bf16[24]{0:T(256)(128)(2,1)S(1)}, bf16[24]{0:T(256)(128)(2,1)}, u32[]{:S(2)}) copy-start(bf16[24]{0:T(256)(128)(2,1)} %param.28) | copy-start | bytes 148
  7.2 16.9 %copy-start.81 = (bf16[24]{0:T(256)(128)(2,1)S(1)}, bf16[24]{0:T(256)(128)(2,1)}, u32[]{:S(2)}) copy-start(bf16[24]{0:T(256)(128)(2,1)} %param.27) | copy-start | bytes 148
  7.2 16.9 %copy-start.80 = (bf16[24]{0:T(256)(128)(2,1)S(1)}, bf16[24]{0:T(256)(128)(2,1)}, u32[]{:S(2)}) copy-start(bf16[24]{0:T(256)(128)(2,1)} %param.26) | copy-start | bytes 148
  7.2 16.9 %copy-start.79 = (bf16[24]{0:T(256)(128)(2,1)S(1)}, bf16[24]{0:T(256)(128)(2,1)}, u32[]{:S(2)}) copy-start(bf16[24]{0:T(256)(128)(2,1)} %param.25) | copy-start | bytes 148
  7.3 168.9 %copy-start.14 = (bf16[128,768]{1,0:T(8,128)(2,1)S(1)}, bf16[128,768]{1,0:T(8,128)(2,1)}, u32[]{:S(2)}) copy-start(bf16[128,768]{1,0:T(8,128)(2,1)} %param.20) | copy-start | bytes 589828
  7.3 204.9 %all-gather.5.cloned.1.call-start = ((), (), s32[]{:S(2)}) async-start(), calls=%async_computation.8 | async-start | bytes 3649536 | tf_op jit(solution)/shard_map/all_gather | solution.py:417
  15.9 195.1 %all-to-all-start.1 = ((bf16[8,40,768]{2,1,0:T(8,128)(2,1)}), bf16[8,40,768]{2,1,0:T(8,128)(2,1)S(1)}, u32[]{:S(2)}, u32[]{:S(2)}) async-start(bf16[8,40,768]{2,1,0:T(8,128)(2,1)} %bitcast.24), calls=%async_computation.1 | async-start | bytes 983040 | tf_op jit(solution)/shard_map/all_to_all | solution.py:436
  23.1 199.3 %all-gather.7.cloned.1.call-start = ((), (), s32[]{:S(2)}) async-start(), calls=%async_computation.9 | async-start | bytes 1216512 | tf_op jit(solution)/shard_map/all_gather | solution.py:418
  23.9 219.3 %all-gather.11.cloned.1.call-start = ((), (), s32[]{:S(2)}) async-start(), calls=%async_computation.11 | async-start | bytes 2457600 | tf_op jit(solution)/shard_map/all_gather | solution.py:437
  24.2 153.6 %copy-start.56 = (s32[64,64]{0,1:T(8,128)}, s32[64,64]{0,1:T(8,128)S(1)}, u32[]{:S(2)}) copy-start(s32[64,64]{0,1:T(8,128)S(1)} %fusion.118) | copy-start | bytes 49156
  187.6 7.0 %copy-start.42 = (f32[2,12,64,64]{2,3,1,0:T(8,128)}, f32[2,12,64,64]{2,3,1,0:T(8,128)S(1)}, u32[]{:S(2)}) copy-start(f32[2,12,64,64]{2,3,1,0:T(8,128)S(1)} %fusion.44) | copy-start | bytes 1179652
  194.6 13.0 %copy-start.6 = (f32[128,768]{1,0:T(8,128)}, f32[128,768]{1,0:T(8,128)S(1)}, u32[]{:S(2)}) copy-start(f32[128,768]{1,0:T(8,128)S(1)} %get-tuple-element.86) | copy-start | bytes 1179652
  194.8 12.1 %copy-start.23 = (bf16[128,768]{1,0:T(8,128)(2,1)}, bf16[128,768]{1,0:T(8,128)(2,1)S(1)}, u32[]{:S(2)}) copy-start(bf16[128,768]{1,0:T(8,128)(2,1)S(1)} %multiply_convert_fusion.8) | copy-start | bytes 589828
  198.1 8.8 %copy-start.21 = (f32[128,3072]{1,0:T(8,128)}, f32[128,3072]{1,0:T(8,128)S(1)}, u32[]{:S(2)}) copy-start(f32[128,3072]{1,0:T(8,128)S(1)} %fusion.135) | copy-start | bytes 4718596
  198.1 8.9 %copy-start.63 = (bf16[32,12]{1,0:T(8,128)(2,1)S(1)}, bf16[32,12]{1,0:T(8,128)(2,1)}, u32[]{:S(2)}) copy-start(bf16[32,12]{1,0:T(8,128)(2,1)} %get-tuple-element.75) | copy-start | bytes 2308
  198.1 8.9 %copy-start.62 = (f32[32,24]{1,0:T(8,128)S(1)}, f32[32,24]{1,0:T(8,128)}, u32[]{:S(2)}) copy-start(f32[32,24]{1,0:T(8,128)} %get-tuple-element.71) | copy-start | bytes 9220
  198.1 9.0 %copy-start.61 = (f32[32,24]{1,0:T(8,128)S(1)}, f32[32,24]{1,0:T(8,128)}, u32[]{:S(2)}) copy-start(f32[32,24]{1,0:T(8,128)} %get-tuple-element.72) | copy-start | bytes 9220
  210.9 11.5 %copy-start.2 = (f32[128,768]{1,0:T(8,128)}, f32[128,768]{1,0:T(8,128)S(1)}, u32[]{:S(2)}) copy-start(f32[128,768]{1,0:T(8,128)S(1)} %get-tuple-element.89) | copy-start | bytes 1179652
  211.8 53.0 %all-gather.9.cloned.1.call-start = ((), (), s32[]{:S(2)}) async-start(), calls=%async_computation.10 | async-start | bytes 2457600 | tf_op jit(solution)/shard_map/all_gather | solution.py:437
  222.4 20.8 %copy-start.45 = (bf16[128,768]{0,1:T(8,128)(2,1)}, bf16[128,768]{0,1:T(8,128)(2,1)S(1)}, u32[]{:S(2)}) copy-start(bf16[128,768]{0,1:T(8,128)(2,1)S(1)} %convert_element_type.273) | copy-start | bytes 589828
  224.2 113.1 %copy-start.8 = (f32[128,768]{1,0:T(8,128)}, f32[128,768]{1,0:T(8,128)S(1)}, u32[]{:S(2)}) copy-start(f32[128,768]{1,0:T(8,128)S(1)} %get-tuple-element.93) | copy-start | bytes 1179652
  224.2 19.0 %copy-start.72 = (f32[128]{0:T(128)}, f32[128]{0:T(128)S(1)}, u32[]{:S(2)}) copy-start(f32[128]{0:T(128)S(1)} %add_rsqrt_fusion) | copy-start | bytes 1540
  243.2 70.6 %reduce-scatter.13.cloned.1.call-start = ((), (), s32[]{:S(2)}) async-start(), calls=%async_computation.14 | async-start | bytes 2457600
  264.8 9.8 %slice-start.4 = ((s8[4718592]{0:T(1024)(128)(4,1)}), s8[4194304]{0:T(1024)(128)(4,1)S(1)}, s32[]{:S(2)}) async-start(s8[4718592]{0:T(1024)(128)(4,1)} %bitcast.262), calls=%async_computation.20 | async-start | bytes 8388608
  264.8 13.0 %slice-start.2 = ((s8[4718592]{0:T(1024)(128)(4,1)}), s8[4194304]{0:T(1024)(128)(4,1)S(1)}, s32[]{:S(2)}) async-start(s8[4718592]{0:T(1024)(128)(4,1)} %bitcast.260), calls=%async_computation.18 | async-start | bytes 8388608
  268.1 9.8 %slice-start.3 = ((s8[4718592]{0:T(1024)(128)(4,1)}), s8[524288]{0:T(1024)(128)(4,1)S(1)}, s32[]{:S(2)}) async-start(s8[4718592]{0:T(1024)(128)(4,1)} %bitcast.260), calls=%async_computation.19 | async-start | bytes 1048576
  294.5 26.7 %copy-start.54 = (s32[128,2]{1,0:T(8,128)S(1)}, s32[128,2]{1,0:T(8,128)}, u32[]{:S(2)}) copy-start(s32[128,2]{1,0:T(8,128)} %get-tuple-element.69) | copy-start | bytes 3076
  294.5 42.0 %copy-start.73 = (f32[128]{0:T(128)S(1)}, f32[128]{0:T(128)}, u32[]{:S(2)}) copy-start(f32[128]{0:T(128)} %copy-done.72) | copy-start | bytes 1540
  315.7 19.4 %all-to-all-start.2 = ((bf16[8,40,768]{2,1,0:T(8,128)(2,1)}), bf16[8,40,768]{2,1,0:T(8,128)(2,1)}, u32[]{:S(2)}, u32[]{:S(2)}) async-start(bf16[8,40,768]{2,1,0:T(8,128)(2,1)} %copy.167), calls=%async_computation.2 | async-start | bytes 983040 | tf_op jit(solution)/shard_map/all_to_all | solution.py:447
  321.2 114.4 %reduce-scatter.11.cloned.1.call-start = ((), (), s32[]{:S(2)}) async-start(), calls=%async_computation.13 | async-start | bytes 1216512 | tf_op jit(solution)/shard_map/reduce_scatter | solution.py:488
  321.3 16.0 %copy-start.77 = (s32[128,2]{0,1:T(2,128)}, s32[128,2]{0,1:T(2,128)S(1)}, u32[]{:S(2)}) copy-start(s32[128,2]{0,1:T(2,128)S(1)} %copy.157) | copy-start | bytes 3076
  338.4 22.0 %copy-start.20 = (f32[128,768]{1,0:T(8,128)}, f32[128,768]{1,0:T(8,128)S(1)}, u32[]{:S(2)}) copy-start(f32[128,768]{1,0:T(8,128)S(1)} %multiply_add_fusion.2) | copy-start | bytes 1179652
  341.1 126.9 %reduce-scatter.15.cloned.1.call-start = ((), (), s32[]{:S(2)}) async-start(), calls=%async_computation.15 | async-start | bytes 2457600
  346.1 317.0 %reduce-scatter.9.cloned.1.call-start = ((), (), s32[]{:S(2)}) async-start(), calls=%async_computation.12 | async-start | bytes 3649536 | tf_op jit(solution)/shard_map/reduce_scatter | solution.py:488
  346.1 8.1 %copy-start.4 = (bf16[4,32,10,768]{3,0,2,1:T(4,128)(2,1)S(1)}, bf16[4,32,10,768]{3,0,2,1:T(4,128)(2,1)}, u32[]{:S(2)}) copy-start(bf16[4,32,10,768]{3,0,2,1:T(4,128)(2,1)} %copy-done.3) | copy-start | bytes 5898244
  346.1 8.1 %copy-start.31 = (bf16[4,320,768]{2,1,0:T(8,128)(2,1)S(1)}, bf16[4,320,768]{2,1,0:T(8,128)(2,1)}, u32[]{:S(2)}) copy-start(bf16[4,320,768]{2,1,0:T(8,128)(2,1)} %copy-done.30) | copy-start | bytes 5898244
  354.3 7.4 %copy-start.60 = (f32[2,12,64]{2,1,0:T(8,128)S(1)}, f32[2,12,64]{2,1,0:T(8,128)}, u32[]{:S(2)}) copy-start(f32[2,12,64]{2,1,0:T(8,128)} %get-tuple-element.90) | copy-start | bytes 18436
  366.1 18.3 %copy-start.1 = (bf16[768,2304]{1,0:T(8,128)(2,1)S(1)}, bf16[768,2304]{1,0:T(8,128)(2,1)}, u32[]{:S(2)}) copy-start(bf16[768,2304]{1,0:T(8,128)(2,1)} %all-gather.5.cloned.1.call-done) | copy-start | bytes 10616836
  390.9 89.2 %copy-start.16 = (f32[128,768]{1,0:T(8,128)}, f32[128,768]{1,0:T(8,128)S(1)}, u32[]{:S(2)}) copy-start(f32[128,768]{1,0:T(8,128)S(1)} %multiply_add_fusion.1) | copy-start | bytes 1179652
  390.9 77.1 %copy-start.22 = (f32[128,3072]{1,0:T(8,128)S(1)}, f32[128,3072]{1,0:T(8,128)}, u32[]{:S(2)}) copy-start(f32[128,3072]{1,0:T(8,128)} %copy-done.21) | copy-start | bytes 4718596
  395.3 77.9 %slice-start = ((s8[4718592]{0:T(1024)(128)(4,1)}), s8[524288]{0:T(1024)(128)(4,1)S(1)}, s32[]{:S(2)}) async-start(s8[4718592]{0:T(1024)(128)(4,1)} %bitcast.228), calls=%async_computation.16 | async-start | bytes 1048576
  473.1 6.9 %copy-start.10 = (bf16[128,3072]{1,0:T(8,128)(2,1)}, bf16[128,3072]{1,0:T(8,128)(2,1)S(1)}, u32[]{:S(2)}) copy-start(bf16[128,3072]{1,0:T(8,128)(2,1)S(1)} %get-tuple-element.62) | copy-start | bytes 2359300
  480.1 8.2 %copy-start.59 = (f32[2,12,64]{2,1,0:T(8,128)S(1)}, f32[2,12,64]{2,1,0:T(8,128)}, u32[]{:S(2)}) copy-start(f32[2,12,64]{2,1,0:T(8,128)} %copy-done.58) | copy-start | bytes 18436
  481.5 8.5 %copy-start.41 = (f32[2,12,64,64]{2,3,1,0:T(8,128)S(1)}, f32[2,12,64,64]{2,3,1,0:T(8,128)}, u32[]{:S(2)}) copy-start(f32[2,12,64,64]{2,3,1,0:T(8,128)} %get-tuple-element.84) | copy-start | bytes 1179652
  481.5 8.5 %copy-start.48 = (bf16[2,64,1,12,64]{1,0,4,3,2:T(2,128)(2,1)S(1)}, bf16[2,64,1,12,64]{1,0,4,3,2:T(2,128)(2,1)}, u32[]{:S(2)}) copy-start(bf16[2,64,1,12,64]{1,0,4,3,2:T(2,128)(2,1)} %get-tuple-element.67) | copy-start | bytes 589828
  481.6 179.3 %all-to-all-start.3 = ((bf16[8,40,768]{2,1,0:T(8,128)(2,1)}), bf16[8,40,768]{2,1,0:T(8,128)(2,1)}, u32[]{:S(2)}, u32[]{:S(2)}) async-start(bf16[8,40,768]{2,1,0:T(8,128)(2,1)} %copy.184), calls=%async_computation.3 | async-start | bytes 983040 | tf_op jit(solution)/shard_map/all_to_all | solution.py:447
  493.3 17.0 %copy-start = (bf16[2,2,2,2,2,24,2304]{6,5,4,3,2,1,0:T(8,128)(2,1)S(1)}, bf16[2,2,2,2,2,24,2304]{6,5,4,3,2,1,0:T(8,128)(2,1)}, u32[]{:S(2)}) copy-start(bf16[2,2,2,2,2,24,2304]{6,5,4,3,2,1,0:T(8,128)(2,1)} %get-tuple-element.34) | copy-start | bytes 10616836
  493.3 17.0 %copy-start.68 = (f32[128]{0:T(128)S(1)}, f32[128]{0:T(128)}, u32[]{:S(2)}) copy-start(f32[128]{0:T(128)} %copy-done.67) | copy-start | bytes 1540
  514.1 7.8 %copy-start.13 = (bf16[128,3072]{1,0:T(8,128)(2,1)S(1)}, bf16[128,3072]{1,0:T(8,128)(2,1)}, u32[]{:S(2)}) copy-start(bf16[128,3072]{1,0:T(8,128)(2,1)} %copy-done.12) | copy-start | bytes 2359300
  514.1 7.8 %copy-start.24 = (bf16[128,768]{1,0:T(8,128)(2,1)S(1)}, bf16[128,768]{1,0:T(8,128)(2,1)}, u32[]{:S(2)}) copy-start(bf16[128,768]{1,0:T(8,128)(2,1)} %copy-done.23) | copy-start | bytes 589828
  533.3 123.8 %copy-start.85 = (f32[128]{0:T(128)S(1)}, f32[128]{0:T(128)}, u32[]{:S(2)}) copy-start(f32[128]{0:T(128)} %get-tuple-element.58) | copy-start | bytes 1540
  533.3 126.6 %copy-start.15 = (bf16[128,768]{1,0:T(8,128)(2,1)S(1)}, bf16[128,768]{1,0:T(8,128)(2,1)}, u32[]{:S(2)}) copy-start(bf16[128,768]{1,0:T(8,128)(2,1)} %param.20) | copy-start | bytes 589828
  533.4 126.6 %copy-start.19 = (f32[128,768]{1,0:T(8,128)S(1)}, f32[128,768]{1,0:T(8,128)}, u32[]{:S(2)}) copy-start(f32[128,768]{1,0:T(8,128)} %copy-done.18) | copy-start | bytes 1179652
  533.4 126.6 %copy-start.46 = (f32[128,768]{1,0:T(8,128)S(1)}, f32[128,768]{1,0:T(8,128)}, u32[]{:S(2)}) copy-start(f32[128,768]{1,0:T(8,128)} %get-tuple-element.101) | copy-start | bytes 1179652
  533.4 127.5 %copy-start.75 = (f32[128,2]{0,1:T(2,128)S(1)}, f32[128,2]{0,1:T(2,128)}, u32[]{:S(2)}) copy-start(f32[128,2]{0,1:T(2,128)} %copy-done.74) | copy-start | bytes 3076
  533.4 127.5 %copy-start.78 = (s32[128,2]{0,1:T(2,128)S(1)}, s32[128,2]{0,1:T(2,128)}, u32[]{:S(2)}) copy-start(s32[128,2]{0,1:T(2,128)} %copy-done.77) | copy-start | bytes 3076
  533.4 129.0 %copy-start.9 = (f32[128,768]{1,0:T(8,128)S(1)}, f32[128,768]{1,0:T(8,128)}, u32[]{:S(2)}) copy-start(f32[128,768]{1,0:T(8,128)} %copy-done.8) | copy-start | bytes 1179652
  657.1 7.6 %copy-start.55 = (f32[24,2304]{1,0:T(8,128)S(1)}, f32[24,2304]{1,0:T(8,128)}, u32[]{:S(2)}) copy-start(f32[24,2304]{1,0:T(8,128)} %get-tuple-element.127) | copy-start | bytes 663556
  657.1 8.3 %copy-start.57 = (f32[24,768]{1,0:T(8,128)S(1)}, f32[24,768]{1,0:T(8,128)}, u32[]{:S(2)}) copy-start(f32[24,768]{1,0:T(8,128)} %get-tuple-element.128) | copy-start | bytes 221188
  657.1 9.0 %copy-start.53 = (f32[24,3072]{1,0:T(8,128)S(1)}, f32[24,3072]{1,0:T(8,128)}, u32[]{:S(2)}) copy-start(f32[24,3072]{1,0:T(8,128)} %get-tuple-element.129) | copy-start | bytes 884740
  657.1 9.7 %copy-start.52 = (f32[24,3072]{1,0:T(8,128)S(1)}, f32[24,3072]{1,0:T(8,128)}, u32[]{:S(2)}) copy-start(f32[24,3072]{1,0:T(8,128)} %get-tuple-element.130) | copy-start | bytes 884740
  657.1 10.4 %copy-start.51 = (f32[96,768]{1,0:T(8,128)S(1)}, f32[96,768]{1,0:T(8,128)}, u32[]{:S(2)}) copy-start(f32[96,768]{1,0:T(8,128)} %get-tuple-element.131) | copy-start | bytes 884740
  (39 other events, 143.2 us)
Sparse Core Ops, SparseCore 0:
  11.0 88.2 all-gather.4
  102.2 55.9 all-gather.6
  212.0 20.8 all-gather.10
  243.3 21.5 all-gather.8
  283.1 30.6 reduce-scatter.12
  341.2 94.3 reduce-scatter.10
  438.3 29.6 reduce-scatter.14
  473.4 106.3 reduce-scatter.8
